TPU v7x, 32 devices: a whole 2x2x4 slice. The times are simulated.
32 devices in a mesh: depth: 8 (over z, core), slab: 4 (over y, x).
Axes of the slice: x: 2, y: 2, z: 4, core: 2. Of those that a mesh axis runs over, the one named last changes fastest.
Arguments:
- state: float32 [8, 2, 2048, 2048], P('depth', None, 'slab'), may hold values from -6 to 6
- fresh: float32 [2, 2, 2048, 2048], P(None, None, 'slab'), may hold values from -6 to 6
- operators: float32 [4, 2, 2, 384, 128], replicated
- band: int32 [8], P('depth'), may hold values from 0 to 1
- freq_sched: int32 [10], replicated, may hold values from 0 to 3
Outputs:
- state_out: float32 [8, 2, 2048, 2048], P('depth', None, 'slab')
- image: float32 [8, 2048], P('depth', 'slab')
All inputs are finite; a program needn't handle non-finite values.
Results may differ from a plain program's by a relative error of at most 0.00011.
Values sent between devices are 32-bit elements; how exact they have to be, the bound alone decides.
No kernel may reach another device: no remote copies, remote signals or barrier semaphores. Data moves between devices by JAX's collectives and lax.ppermute only.
A program may use at most 192 MiB of HBM per device.

v0:
```python
import jax
import jax.numpy as jnp
from jax import lax
from jax.sharding import PartitionSpec as P


def extended_2(value, sides, width):
    for axis, dim in sides:
        peers, length = (lax.axis_size(axis), value.shape[dim])
        up = [(i, (i + 1) % peers) for i in range(peers - 1)]
        down = [(j, i) for i, j in up]
        last = lax.slice_in_dim(value, length - width, length, axis=dim)
        first = lax.slice_in_dim(value, 0, width, axis=dim)
        before = lax.ppermute(last, axis, up)
        after = lax.ppermute(first, axis, down)
        value = jnp.concatenate([before, value, after], axis=dim)
    return value


def passed_along(value, axis, steps):
    count = lax.axis_size(axis)
    first, last = (max(0, -steps), min(count, count - steps))
    return lax.ppermute(value, axis, [(source, source + steps) for source in range(first, last)])


def real_form(operator):
    upper_rows = jnp.concatenate([operator[0], operator[1]], axis=1)
    lower_rows = jnp.concatenate([-operator[1], operator[0]], axis=1)
    return jnp.concatenate([upper_rows, lower_rows], axis=0)


def along_middle(extended, combined, width):
    count = extended.shape[1] // width - 2
    blocks = extended.reshape(2, count + 2, width, extended.shape[2])
    triple = jnp.concatenate(
        [
            blocks[0, :-2],
            blocks[0, 1:-1],
            blocks[0, 2:],
            blocks[1, :-2],
            blocks[1, 1:-1],
            blocks[1, 2:],
        ],
        axis=1,
    )
    output = jnp.einsum("bic,ij->bjc", triple, combined, precision=lax.Precision.HIGHEST)
    real_part = output[:, :width].reshape(count * width, extended.shape[2])
    imag_part = output[:, width:].reshape(count * width, extended.shape[2])
    return jnp.stack([real_part, imag_part])


def along_last(field, combined, width):
    count = field.shape[2] // width
    padded = jnp.pad(field, ((0, 0), (0, 0), (width, width)))
    blocks = padded.reshape(2, field.shape[1], count + 2, width)
    triple = jnp.concatenate(
        [
            blocks[0, :, :-2],
            blocks[0, :, 1:-1],
            blocks[0, :, 2:],
            blocks[1, :, :-2],
            blocks[1, :, 1:-1],
            blocks[1, :, 2:],
        ],
        axis=2,
    )
    output = jnp.einsum("abi,ij->abj", triple, combined, precision=lax.Precision.HIGHEST)
    real_part = output[:, :, :width].reshape(field.shape[1], count * width)
    imag_part = output[:, :, width:].reshape(field.shape[1], count * width)
    return jnp.stack([real_part, imag_part])


def across_shots(field, combined, width):
    extended = extended_2(field, (("slab", 1),), width)
    return along_middle(extended, combined, width)


def advance(field, operator):
    width = operator.shape[-1]
    combined = real_form(operator)
    return across_shots(along_last(field, combined, width), combined, width)


def body(state, fresh, operators, band, freq_sched):
    owner = lax.axis_index("depth")
    slab_index = lax.axis_index("slab")
    current = state[0]
    rows = current.shape[1]
    ticks = fresh.shape[0]
    image = jnp.zeros((1, rows), jnp.float32)
    for tick in range(ticks):
        freq_id = freq_sched[ticks - tick + owner]
        operator = operators[freq_id, band[0]]
        result = advance(current, operator)
        square = lax.dynamic_slice_in_dim(result[0], slab_index * rows, rows, 1)
        image = image + jnp.diagonal(square)[None]
        moved = passed_along(result, "depth", 1)
        current = jnp.where(owner == 0, fresh[tick], moved)
    return (current[None], image)


def solution(mesh):
    return jax.shard_map(
        body,
        mesh=mesh,
        in_specs=(
            P("depth", None, "slab", None),
            P(None, None, "slab", None),
            P(),
            P("depth"),
            P(),
        ),
        out_specs=(P("depth", None, "slab", None), P("depth", "slab")),
        check_vma=False,
    )
```

profile of v0, /device:TPU:1, one launch (start us, length us, event | category | flops | bytes accessed | tf_op | source)
XLA Modules:
  0.0 793.8 jit_solution(7292617094698292471)
XLA Ops:
  8.1 8.7 %copy.15 = f32[1,2,512,2048]{2,3,1,0:T(8,128)} copy(f32[1,2,512,2048]{3,2,1,0:T(8,128)} %param.5) | data formatting | bytes 16777216 | tf_op args[0]
  16.7 8.2 %pad.7 = f32[2,512,2304]{1,2,0:T(8,128)} pad(f32[2,512,2048]{1,2,0:T(8,128)} %bitcast.149, f32[]{:T(128)} %constant.31.clone.1), padding=0_0x0_0x128_128 | pad | bytes 17825796 | tf_op jit(solution)/shard_map/jit(_pad)/pad | solution.py:54
  24.9 17.7 %fusion.21 = (f32[1,512,16,128]{1,3,2,0:T(8,128)}, f32[1,512,16,128]{1,3,2,0:T(8,128)}, f32[1,512,16,128]{1,3,2,0:T(8,128)}, f32[1,512,16,128]{1,3,2,0:T(8,128)}...) fusion(f32[2,512,18,128]{1,3,2,0:T(8,128)} %bitcast.128), kind=kLoop, calls=%fused_computation.70 | loop fusion | bytes 50331648 | tf_op jit(solution)/shard_map/slice | solution.py:63
  42.6 5.3 copy.43
  48.0 4.8 bitcast_dynamic-update-slice_fusion.11
  52.8 5.4 copy.44
  58.1 5.3 copy.45
  63.5 5.4 copy.46
  68.8 5.4 copy.47
  74.2 5.3 copy.48
  79.5 4.9 bitcast_dynamic-update-slice_fusion.10
  84.4 2.4 bitcast_dynamic-update-slice_fusion.9
  86.8 2.5 bitcast_dynamic-update-slice_fusion.8
  89.3 2.5 bitcast_dynamic-update-slice_fusion.7
  94.8 26.0 %fusion.13 = f32[512,16,256]{0,2,1:T(8,128)S(1)} fusion(f32[512,16,768]{2,0,1:T(8,128)} %bitcast_dynamic-update-slice_fusion.6, f32[384,128]{0,1:T(8,128)S(1)} %bitcast.162, f32[384,128]{0,1:T(8,128)S(1)} %bitcast_negate_fusion, f32[384,128]{0,1:T(8,128)S(1)} %bitcast.158), kind=kOutput, calls=%fused_computation.53 | convolution fusion | flops 19327942656 | bytes 34144256 | tf_op jit(solution)/shard_map/abi,ij->abj/dot_general | solution.py:67
  122.6 4.1 collective-permute-start
  128.0 42.8 %collective-permute-done = f32[2,128,2048]{1,2,0:T(8,128)S(1)} collective-permute-done((f32[2,128,2048]{1,2,0:T(8,128)S(1)}, f32[2,128,2048]{1,2,0:T(8,128)S(1)}, u32[]{:S(2)}, u32[]{:S(2)}) %collective-permute-start) | collective-permute-done | bytes 2097184 | tf_op jit(solution)/shard_map/ppermute | solution.py:14
  170.9 46.9 %collective-permute-done.1 = f32[2,128,2048]{1,2,0:T(8,128)S(1)} collective-permute-done((f32[2,128,2048]{1,2,0:T(8,128)S(1)}, f32[2,128,2048]{1,2,0:T(8,128)S(1)}, u32[]{:S(2)}, u32[]{:S(2)}) %collective-permute-start.1) | collective-permute-done | bytes 2097184 | tf_op jit(solution)/shard_map/ppermute | solution.py:15
  217.7 5.0 pad_maximum_fusion
  222.8 12.8 %copy.22 = f32[2,768,2048]{2,1,0:T(8,128)} copy(f32[2,768,2048]{1,2,0:T(8,128)} %pad_maximum_fusion) | data formatting | bytes 25165824 | tf_op jit(solution)/shard_map/concatenate | solution.py:16
  235.5 2.6 fusion.12
  238.1 2.8 fusion.11
  244.6 24.2 %convolution_bitcast_fusion.1 = f32[4,256,2048]{2,1,0:T(8,128)} fusion(f32[4,768,2048]{2,1,0:T(8,128)S(1)} %fusion.7, f32[384,128]{0,1:T(8,128)S(1)} %bitcast.163, f32[384,128]{0,1:T(8,128)S(1)} %bitcast_negate_fusion, f32[384,128]{0,1:T(8,128)S(1)} %bitcast.159), kind=kOutput, calls=%fused_computation.10 | convolution fusion | flops 19327942656 | bytes 34144256 | tf_op jit(solution)/shard_map/bic,ij->bjc/dot_general | solution.py:46
  268.8 7.9 fusion.24
  276.7 5.4 copy.23
  282.0 5.6 copy.24
  287.6 7.8 pad_maximum_fusion.2
  295.5 4.6 collective-permute-start.2
  300.1 10.8 %fusion.19 = (f32[1,2,512,2048]{3,2,1,0:T(8,128)}, f32[1,2,512,2048]{3,2,1,0:T(8,128)}) fusion(f32[2,2,512,2048]{3,2,1,0:T(8,128)} %param.6), kind=kLoop, calls=%fused_computation.68 | loop fusion | bytes 33554432 | tf_op jit(solution)/shard_map/slice | solution.py:98
  311.0 8.8 %copy.39 = f32[1,2,512,2048]{2,3,1,0:T(8,128)} copy(f32[1,2,512,2048]{3,2,1,0:T(8,128)} %get-tuple-element.5) | data formatting | bytes 16777216
  320.0 70.8 %collective-permute-done.2 = f32[2,512,2048]{1,2,0:T(8,128)} collective-permute-done((f32[2,512,2048]{1,2,0:T(8,128)}, f32[2,512,2048]{1,2,0:T(8,128)}, u32[]{:S(2)}, u32[]{:S(2)}) %collective-permute-start.2) | collective-permute-done | bytes 8388640 | tf_op jit(solution)/shard_map/ppermute | solution.py:23
  390.8 11.3 %bitcast_select_fusion = f32[2,512,2048]{1,2,0:T(8,128)} fusion(f32[2,512,2048]{1,2,0:T(8,128)} %collective-permute-done.2, f32[1,2,512,2048]{2,3,1,0:T(8,128)} %copy.39, pred[]{:T(512)S(6)} %eq.4), kind=kLoop, calls=%fused_computation.6 | loop fusion | flops 2097152 | bytes 25165824 | tf_op jit(solution)/shard_map/jit(_where)/select_n | solution.py:98
  402.1 8.2 %pad.8 = f32[2,512,2304]{1,2,0:T(8,128)} pad(f32[2,512,2048]{1,2,0:T(8,128)} %bitcast_select_fusion, f32[]{:T(128)} %constant.31.clone.1), padding=0_0x0_0x128_128 | pad | bytes 17825796 | tf_op jit(solution)/shard_map/jit(_pad)/pad | solution.py:54
  410.2 17.7 %fusion.20 = (f32[1,512,16,128]{1,3,2,0:T(8,128)}, f32[1,512,16,128]{1,3,2,0:T(8,128)}, f32[1,512,16,128]{1,3,2,0:T(8,128)}, f32[1,512,16,128]{1,3,2,0:T(8,128)}...) fusion(f32[2,512,18,128]{1,3,2,0:T(8,128)} %bitcast.127), kind=kLoop, calls=%fused_computation.69 | loop fusion | bytes 50331648 | tf_op jit(solution)/shard_map/slice | solution.py:63
  427.9 5.3 copy.49
  433.2 4.8 bitcast_dynamic-update-slice_fusion.5
  438.0 5.4 copy.50
  443.4 5.4 copy.51
  448.8 5.3 copy.52
  454.1 5.3 copy.53
  459.4 5.4 copy.54
  464.8 4.9 bitcast_dynamic-update-slice_fusion.4
  472.2 2.5 bitcast_dynamic-update-slice_fusion.2
  474.7 2.5 bitcast_dynamic-update-slice_fusion.1
  480.1 25.9 %fusion.14 = f32[512,16,256]{0,2,1:T(8,128)S(1)} fusion(f32[512,16,768]{2,0,1:T(8,128)} %bitcast_dynamic-update-slice_fusion, f32[384,128]{0,1:T(8,128)S(1)} %bitcast.160, f32[384,128]{0,1:T(8,128)S(1)} %bitcast_negate_fusion.1, f32[384,128]{0,1:T(8,128)S(1)} %bitcast.156), kind=kOutput, calls=%fused_computation.54 | convolution fusion | flops 19327942656 | bytes 34144256 | tf_op jit(solution)/shard_map/abi,ij->abj/dot_general | solution.py:67
  507.9 3.3 collective-permute-start.3
  512.4 21.5 %collective-permute-done.3 = f32[2,128,2048]{1,2,0:T(8,128)S(1)} collective-permute-done((f32[2,128,2048]{1,2,0:T(8,128)S(1)}, f32[2,128,2048]{1,2,0:T(8,128)S(1)}, u32[]{:S(2)}, u32[]{:S(2)}) %collective-permute-start.3) | collective-permute-done | bytes 2097184 | tf_op jit(solution)/shard_map/ppermute | solution.py:14
  534.0 22.9 %collective-permute-done.4 = f32[2,128,2048]{1,2,0:T(8,128)S(1)} collective-permute-done((f32[2,128,2048]{1,2,0:T(8,128)S(1)}, f32[2,128,2048]{1,2,0:T(8,128)S(1)}, u32[]{:S(2)}, u32[]{:S(2)}) %collective-permute-start.4) | collective-permute-done | bytes 2097184 | tf_op jit(solution)/shard_map/ppermute | solution.py:15
  556.9 5.0 pad_maximum_fusion.1
  561.9 12.8 %copy.31 = f32[2,768,2048]{2,1,0:T(8,128)} copy(f32[2,768,2048]{1,2,0:T(8,128)} %pad_maximum_fusion.1) | data formatting | bytes 25165824 | tf_op jit(solution)/shard_map/concatenate | solution.py:16
  574.7 2.6 fusion.6
  577.3 2.8 fusion.5
  583.8 24.0 %convolution_bitcast_fusion = f32[4,256,2048]{2,1,0:T(8,128)} fusion(f32[4,768,2048]{2,1,0:T(8,128)S(1)} %fusion.1, f32[384,128]{0,1:T(8,128)S(1)} %bitcast.161, f32[384,128]{0,1:T(8,128)S(1)} %bitcast_negate_fusion.1, f32[384,128]{0,1:T(8,128)S(1)} %bitcast.157), kind=kOutput, calls=%fused_computation.9 | convolution fusion | flops 19327942656 | bytes 34144256 | tf_op jit(solution)/shard_map/bic,ij->bjc/dot_general | solution.py:46
  607.8 7.9 fusion.22
  615.7 5.4 copy.32
  621.1 5.5 copy.33
  626.6 7.8 pad_maximum_fusion.3
  634.4 48.7 %collective-permute-start.5 = (f32[2,512,2048]{1,2,0:T(8,128)}, f32[2,512,2048]{1,2,0:T(8,128)}, u32[]{:S(2)}, u32[]{:S(2)}) collective-permute-start(f32[2,512,2048]{1,2,0:T(8,128)} %pad_maximum_fusion.3), channel_id=1, source_target_pairs={{0,4},{4,8},{8,12},{12,16},{16,20},{20,24},{24,28},{1,5},{5,9},{9,... | collective-permute-start | bytes 25165832 | tf_op jit(solution)/shard_map/ppermute | solution.py:23
  683.2 8.7 %copy.35 = f32[1,2,512,2048]{2,3,1,0:T(8,128)} copy(f32[1,2,512,2048]{3,2,1,0:T(8,128)} %get-tuple-element.4) | data formatting | bytes 16777216
  693.1 4.5 gather_fusion
  699.0 4.5 gather_fusion.1
  704.1 69.7 %collective-permute-done.5 = f32[2,512,2048]{1,2,0:T(8,128)} collective-permute-done((f32[2,512,2048]{1,2,0:T(8,128)}, f32[2,512,2048]{1,2,0:T(8,128)}, u32[]{:S(2)}, u32[]{:S(2)}) %collective-permute-start.5) | collective-permute-done | bytes 8388640 | tf_op jit(solution)/shard_map/ppermute | solution.py:23
  773.8 11.1 %fusion = f32[1,2,512,2048]{2,3,1,0:T(8,128)} fusion(f32[2,512,2048]{1,2,0:T(8,128)} %collective-permute-done.5, f32[1,2,512,2048]{2,3,1,0:T(8,128)} %copy.35, pred[]{:T(512)S(6)} %eq.4), kind=kLoop, calls=%fused_computation.8 | loop fusion | flops 2097152 | bytes 25165824 | tf_op jit(solution)/shard_map/broadcast_in_dim | solution.py:99
  784.9 8.7 %copy.34 = f32[1,2,512,2048]{3,2,1,0:T(8,128)} copy(f32[1,2,512,2048]{2,3,1,0:T(8,128)} %fusion) | data formatting | bytes 16777216
  (49 shorter events, 28.4 us)
Async XLA Ops:
  79.5 4.9 copy-start.8
  79.5 7.3 copy-start.6
  84.4 4.9 copy-start.2
  86.8 5.6 copy-start.3
  122.6 48.2 %collective-permute-start = (f32[2,128,2048]{1,2,0:T(8,128)S(1)}, f32[2,128,2048]{1,2,0:T(8,128)S(1)}, u32[]{:S(2)}, u32[]{:S(2)}) collective-permute-start(f32[2,128,2048]{1,2,0:T(8,128)S(1)} %get-tuple-element.26), channel_id=1, source_target_pairs={{0,1},{1,2},{2,3},{4,5},{5,6},{6,7},{8,9},{9,10},{10,11},{12,13},{... | collective-permute-start | bytes 6291464 | tf_op jit(solution)/shard_map/ppermute | solution.py:14
  126.7 91.0 %collective-permute-start.1 = (f32[2,128,2048]{1,2,0:T(8,128)S(1)}, f32[2,128,2048]{1,2,0:T(8,128)S(1)}, u32[]{:S(2)}, u32[]{:S(2)}) collective-permute-start(f32[2,128,2048]{1,2,0:T(8,128)S(1)} %get-tuple-element.27), channel_id=1, source_target_pairs={{1,0},{2,1},{3,2},{5,4},{6,5},{7,6},{9,8},{10,9},{11,10},{13,12},{... | collective-permute-start | bytes 6291464 | tf_op jit(solution)/shard_map/ppermute | solution.py:15
  235.5 7.1 copy-start
  295.5 95.3 %collective-permute-start.2 = (f32[2,512,2048]{1,2,0:T(8,128)}, f32[2,512,2048]{1,2,0:T(8,128)}, u32[]{:S(2)}, u32[]{:S(2)}) collective-permute-start(f32[2,512,2048]{1,2,0:T(8,128)} %pad_maximum_fusion.2), channel_id=1, source_target_pairs={{0,4},{4,8},{8,12},{12,16},{16,20},{20,24},{24,28},{1,5},{5,9},{9,... | collective-permute-start | bytes 25165832 | tf_op jit(solution)/shard_map/ppermute | solution.py:23
  464.8 4.9 copy-start.9
  464.8 7.3 copy-start.7
  469.7 4.9 copy-start.4
  472.2 5.6 copy-start.5
  507.9 26.1 %collective-permute-start.3 = (f32[2,128,2048]{1,2,0:T(8,128)S(1)}, f32[2,128,2048]{1,2,0:T(8,128)S(1)}, u32[]{:S(2)}, u32[]{:S(2)}) collective-permute-start(f32[2,128,2048]{1,2,0:T(8,128)S(1)} %get-tuple-element.20), channel_id=1, source_target_pairs={{0,1},{1,2},{2,3},{4,5},{5,6},{6,7},{8,9},{9,10},{10,11},{12,13},{... | collective-permute-start | bytes 6291464 | tf_op jit(solution)/shard_map/ppermute | solution.py:14
  511.1 45.7 %collective-permute-start.4 = (f32[2,128,2048]{1,2,0:T(8,128)S(1)}, f32[2,128,2048]{1,2,0:T(8,128)S(1)}, u32[]{:S(2)}, u32[]{:S(2)}) collective-permute-start(f32[2,128,2048]{1,2,0:T(8,128)S(1)} %get-tuple-element.21), channel_id=1, source_target_pairs={{1,0},{2,1},{3,2},{5,4},{6,5},{7,6},{9,8},{10,9},{11,10},{13,12},{... | collective-permute-start | bytes 6291464 | tf_op jit(solution)/shard_map/ppermute | solution.py:15
  574.7 7.1 copy-start.1
  634.4 139.4 %collective-permute-start.5 = (f32[2,512,2048]{1,2,0:T(8,128)}, f32[2,512,2048]{1,2,0:T(8,128)}, u32[]{:S(2)}, u32[]{:S(2)}) collective-permute-start(f32[2,512,2048]{1,2,0:T(8,128)} %pad_maximum_fusion.3), channel_id=1, source_target_pairs={{0,4},{4,8},{8,12},{12,16},{16,20},{20,24},{24,28},{1,5},{5,9},{9,... | collective-permute-start | bytes 25165832 | tf_op jit(solution)/shard_map/ppermute | solution.py:23
where the time goes:
time: 801 us; the launch traced here: 794 us
  local copies, waits for them, and re-layouts  301 us (38%)
  waiting for transfers between devices  275 us (34%)
  matrix products  100 us (12%)
  starting transfers between devices  63.3 us (8%)
  other arithmetic  49.3 us (6%)
    unnamed x60, local copies, waits for them, and re-layouts  152 us
    ppermute x2, waiting for transfers between devices, passed_along(): lax.ppermute(value, axis, [(source, source + steps) for source in range(f...  141 us
    ppermute x2, waiting for transfers between devices, extended_2(): after = lax.ppermute(first, axis, down)  69.8 us
    ppermute x2, waiting for transfers between devices, extended_2(): before = lax.ppermute(last, axis, up)  64.4 us
    ppermute x2, starting transfers between devices, passed_along(): lax.ppermute(value, axis, [(source, source + steps) for source in range(f...  53.3 us
    dot_general x2, matrix products, along_last(): jnp.einsum('abi,ij->abj', triple, combined, precision=lax.Precision.HIGHEST)  51.9 us
    dot_general x2, matrix products, along_middle(): jnp.einsum('bic,ij->bjc', triple, combined, precision=lax.Precision.HIGHEST)  48.2 us
    slice x2, local copies, waits for them, and re-layouts, along_last(): blocks[1, :, 2:]  35.4 us
  transfers between devices with their start and end apart: 6, of which 6 were waited for; matrix products, arithmetic and copies ran while one was open for 5% of the time, Pallas kernels for 0%

commit v1 on v0

v1 whole, which is shorter than its diff:
```python
import functools
import math

import jax
import jax.numpy as jnp
from jax import lax
from jax.experimental import pallas as pl
from jax.experimental.pallas import tpu as pltpu
from jax.sharding import PartitionSpec as P

BF = jnp.bfloat16
F32 = jnp.float32
VMEM = 62 << 20
AXES = ("depth", "slab")


def split(value):
    high = value.astype(BF)
    return high, (value - high.astype(F32)).astype(BF)


def params():
    return pltpu.CompilerParams(vmem_limit_bytes=VMEM)


def after(value, *others):
    return lax.optimization_barrier((value, *others))[0]


def cost():
    return pl.CostEstimate(flops=1, bytes_accessed=1, transcendentals=0)


def rows_kernel(mode, x_ref, *outs):
    @pl.when(mode[0] == 1)
    def _():
        outs[0][...] = x_ref[...]

    @pl.when(mode[0] == 2)
    def _():
        at = 0
        for ref in outs[1:]:
            ref[...] = x_ref[:, :, at : at + ref.shape[2]]
            at += ref.shape[2]


def rows_of(mode, x, blocks, width, chunks):
    cols = x.shape[-1]
    tall = width // 4
    lengths = [(1, cols)] + [(2, cols // chunks)] * chunks

    def part(wanted, length):
        return pl.BlockSpec((2, tall, length), lambda i, mode: (0, jnp.where(mode[0] == wanted, i, 0), 0))

    return pl.pallas_call(
        rows_kernel,
        grid_spec=pltpu.PrefetchScalarGridSpec(
            num_scalar_prefetch=1,
            grid=(4 * blocks,),
            in_specs=[
                pl.BlockSpec(
                    (None, 2, tall, cols),
                    lambda i, mode: (0, 0, 4 * mode[1] + jnp.where(mode[0] > 0, i, 0), 0),
                )
            ],
            out_specs=[part(*item) for item in lengths],
        ),
        out_shape=[jax.ShapeDtypeStruct((2, blocks * width, length), F32) for _, length in lengths],
        compiler_params=params(),
        cost_estimate=cost(),
    )(mode, x)


def receivers_kernel(mode, *refs, width, nb, group, sources, chunks):
    inputs, (w_ref,), outs = refs[:sources], refs[sources : sources + 1], refs[sources + 1 : sources + 1 + chunks]
    xh, xl, zh, zl = refs[sources + 1 + chunks :]
    rows = inputs[0].shape[1]
    wide = 2 * width
    m = group * rows

    def product(high, low, g, step):
        hi = [high[g * group + t : g * group + t + group].reshape(m, wide) for t in range(3)]
        lo = [low[g * group + t : g * group + t + group].reshape(m, wide) for t in range(3)]
        left = jnp.concatenate(hi + lo + hi, axis=1)
        return jnp.dot(left, w_ref[step], preferred_element_type=F32).reshape(group, rows, wide)

    @pl.when(mode[0] > 0)
    def _():
        zero = jnp.zeros((1, rows, wide), BF)
        for buffer in (xh, xl, zh, zl):
            buffer[0:1] = zero
            buffer[nb + 1 : nb + 2] = zero
        for source, ref in enumerate(inputs):

            @pl.when(mode[0] == source + 1)
            def _(ref=ref):
                for j in range(nb):
                    for p in range(2):
                        high, low = split(ref[p, :, j * width : (j + 1) * width])
                        xh[j + 1, :, p * width : (p + 1) * width] = high
                        xl[j + 1, :, p * width : (p + 1) * width] = low

        for g in range(nb // group):
            high, low = split(product(xh, xl, g, 0))
            zh[g * group + 1 : g * group + 1 + group] = high
            zl[g * group + 1 : g * group + 1 + group] = low
        per = nb // chunks
        for g in range(nb // group):
            y = product(zh, zl, g, 1)
            for j in range(group):
                block = g * group + j
                out, at = outs[block // per], (block % per) * width
                for p in range(2):
                    out[p, :, at : at + width] = y[j, :, p * width : (p + 1) * width]


def receivers(mode, sources, weights, blocks, width, chunks):
    cols = sources[0].shape[-1]
    nb = cols // width
    group = 2 if nb % 2 == 0 else 1
    per = cols // chunks
    in_specs = []
    for number, array in enumerate(sources):
        lead = (None,) * (array.ndim - 3)

        def rows_at(i, mode, number=number, lead=lead):
            first = mode[1] if lead else 0
            return (0,) * len(lead) + (0, first + jnp.where(mode[0] == number + 1, i, 0), 0)

        in_specs.append(pl.BlockSpec((*lead, 2, width, cols), rows_at))
    in_specs.append(pl.BlockSpec(weights.shape, lambda i, mode: (0, 0, 0)))
    return pl.pallas_call(
        functools.partial(receivers_kernel, width=width, nb=nb, group=group, sources=len(sources), chunks=chunks),
        grid_spec=pltpu.PrefetchScalarGridSpec(
            num_scalar_prefetch=1,
            grid=(blocks,),
            in_specs=in_specs,
            out_specs=[pl.BlockSpec((2, width, per), lambda i, mode: (0, jnp.where(mode[0] > 0, i, 0), 0))] * chunks,
            scratch_shapes=[pltpu.VMEM((nb + 2, width, 2 * width), BF)] * 4,
        ),
        out_shape=[jax.ShapeDtypeStruct((2, blocks * width, per), F32)] * chunks,
        compiler_params=params(),
        cost_estimate=cost(),
    )(mode, *sources, weights)


def shots_body(mode, groups, vh_ref, vl_ref, xh, xl, store, width, nb):
    wide = 2 * width
    for number, ref in enumerate(groups):
        for b in range(ref.shape[1] // width):
            for p in range(2):
                high, low = split(ref[p, b * width : (b + 1) * width])
                at = pl.multiple_of((mode[1 + number] + b) * wide + p * width, width)
                xh[pl.ds(at, width)] = high
                xl[pl.ds(at, width)] = low
    for b in range(nb):
        centre = 5 if b == 0 else (6 if b == nb - 1 else 2)
        order = (0, 1, centre, 3, 4)
        high = [vh_ref[k] for k in order]
        low = [vl_ref[k] for k in order]
        left = jnp.concatenate(high + high + low, axis=1)
        h = xh[b * wide : (b + 5) * wide]
        l = xl[b * wide : (b + 5) * wide]
        y = jnp.dot(left, jnp.concatenate([h, l, h], axis=0), preferred_element_type=F32)
        store(b, y)


def shots_kernel(mode, *refs, width, nb, count, fresh):
    groups, rest = refs[:count], refs[count:]
    vh_ref, vl_ref, top_ref = rest[:3]
    o_ref, xh, xl = rest[-3:]

    def store(b, y):
        y = y * top_ref[0:1, 0:1] * top_ref[1:2, 0:1]
        for p in range(2):
            o_ref[p, b * width : (b + 1) * width] = y[p * width : (p + 1) * width]

    @pl.when(mode[0] == 1)
    def _():
        shots_body(mode, groups, vh_ref, vl_ref, xh, xl, store, width, nb)

    if fresh:

        @pl.when(mode[0] == 2)
        def _():
            o_ref[...] = rest[3][...]


def shots(mode, groups, weights, width, nb, at, length, total, fresh=None, into=None):
    vh, vl, tops = weights
    rows = nb * width
    ct = min(2 * width, length)
    start = at // ct

    def columns(array):
        first = 0 if array.shape[-1] == length else start
        lead = (None,) * (array.ndim - 3)
        return pl.BlockSpec(
            (*lead, 2, array.shape[-2], ct),
            lambda i, mode: (0,) * (len(lead) + 2) + (first + jnp.where(mode[0] == 1, i, 0),),
        )

    in_specs = [columns(array) for array in groups]
    in_specs += [pl.BlockSpec(vh.shape, lambda i, mode: (0, 0, 0))] * 2
    in_specs.append(pl.BlockSpec(tops.shape, lambda i, mode: (0, 0)))
    operands = [*groups, vh, vl, tops]
    aliases = {}
    if fresh is not None:
        in_specs.append(
            pl.BlockSpec(
                (None, 2, rows, ct),
                lambda i, mode: (fresh.shape[0] - 1, 0, 0, start + jnp.where(mode[0] == 2, i, 0)),
            )
        )
        operands.append(fresh)
    if into is not None:
        in_specs.append(pl.BlockSpec(memory_space=pl.ANY))
        operands.append(into)
        aliases = {len(operands): 0}
    return pl.pallas_call(
        functools.partial(shots_kernel, width=width, nb=nb, count=len(groups), fresh=fresh is not None),
        grid_spec=pltpu.PrefetchScalarGridSpec(
            num_scalar_prefetch=1,
            grid=(length // ct,),
            in_specs=in_specs,
            out_specs=pl.BlockSpec((2, rows, ct), lambda i, mode: (0, 0, start + jnp.where(mode[0] > 0, i, 0))),
            scratch_shapes=[pltpu.VMEM(((nb + 4) * 2 * width, ct), BF)] * 2,
        ),
        out_shape=jax.ShapeDtypeStruct((2, rows, total), F32),
        input_output_aliases=aliases,
        compiler_params=params(),
        cost_estimate=cost(),
    )(mode, *operands)


def place_kernel(mode, new_ref, old_ref, o_ref):
    @pl.when(mode[0] == 1)
    def _():
        o_ref[...] = new_ref[...]

    @pl.when(mode[0] != 1)
    def _():
        o_ref[...] = old_ref[...]


def place(mode, new, into, at):
    rows, cols = new.shape[1:]
    tall = math.gcd(rows, 32)
    start = at // tall
    return pl.pallas_call(
        place_kernel,
        grid_spec=pltpu.PrefetchScalarGridSpec(
            num_scalar_prefetch=1,
            grid=(rows // tall,),
            in_specs=[
                pl.BlockSpec((2, tall, cols), lambda i, mode: (0, jnp.where(mode[0] == 1, i, 0), 0)),
                pl.BlockSpec((2, tall, cols), lambda i, mode: (0, start, 0)),
            ],
            out_specs=pl.BlockSpec((2, tall, cols), lambda i, mode: (0, start + jnp.where(mode[0] == 1, i, 0), 0)),
        ),
        out_shape=jax.ShapeDtypeStruct(into.shape, F32),
        input_output_aliases={2: 0},
        compiler_params=params(),
        cost_estimate=cost(),
    )(mode, new, into)


def diagonal_kernel(info, x_ref, w_ref, s_ref, c_ref, o_ref, xh, xl, zh, zl, *, width, total):
    r = pl.program_id(0)
    block = info[0] + r
    wide = 2 * width

    def valid(offset):
        at = block + offset
        return ((at >= 0) & (at < total)).astype(F32)

    @pl.when(r == 0)
    def _():
        o_ref[...] = jnp.zeros(o_ref.shape, F32)

    def product(high, low, count, step):
        hi = [high[t : t + count].reshape(count * width, wide) for t in range(3)]
        lo = [low[t : t + count].reshape(count * width, wide) for t in range(3)]
        left = jnp.concatenate(hi + lo + hi, axis=1)
        return jnp.dot(left, w_ref[step], preferred_element_type=F32).reshape(count, width, wide)

    def given(z, m):
        return jnp.sum(z[:, :width] * m[0] - z[:, width:] * m[1], axis=0, keepdims=True)

    @pl.when(info[1] > 0)
    def _():
        for slot in range(9):
            at = jnp.clip(block + slot - 4, 0, total - 1) * width
            for p in range(2):
                value = x_ref[p, :, pl.ds(pl.multiple_of(at, width), width)] * valid(slot - 4)
                high, low = split(value)
                xh[slot, :, p * width : (p + 1) * width] = high
                xl[slot, :, p * width : (p + 1) * width] = low
        z1 = product(xh, xl, 7, 0)
        for offset in (-1, 0, 1):
            o_ref[0, pl.ds(r + 2 + offset, 1), :] += given(z1[offset + 3], s_ref[1 - offset]) * valid(offset)
        for slot in range(7):
            high, low = split(z1[slot] * valid(slot - 3))
            zh[slot] = high
            zl[slot] = low
        z2 = product(zh, zl, 5, 1)
        for offset in (-2, -1, 0, 1, 2):
            o_ref[1, pl.ds(r + 2 + offset, 1), :] += given(z2[offset + 2], c_ref[2 - offset]) * valid(offset)
        for which, edge in ((5, block == 0), (6, block == total - 1)):
            o_ref[1, pl.ds(r + 2, 1), :] -= jnp.where(edge, given(z2[2], c_ref[which]), 0.0)


def diagonal(info, x, weights, single, double, width):
    rows, cols = x.shape[-2:]
    nb, total = rows // width, cols // width
    return pl.pallas_call(
        functools.partial(diagonal_kernel, width=width, total=total),
        grid_spec=pltpu.PrefetchScalarGridSpec(
            num_scalar_prefetch=1,
            grid=(nb,),
            in_specs=[
                pl.BlockSpec((None, 2, width, cols), lambda i, info: (0, 0, jnp.where(info[1] > 0, i, 0), 0)),
                pl.BlockSpec(weights.shape, lambda i, info: (0, 0, 0)),
                pl.BlockSpec(single.shape, lambda i, info: (0, 0, 0, 0)),
                pl.BlockSpec(double.shape, lambda i, info: (0, 0, 0, 0)),
            ],
            out_specs=pl.BlockSpec((2, nb + 4, width), lambda i, info: (0, 0, 0)),
            scratch_shapes=[pltpu.VMEM((9, width, 2 * width), BF)] * 2 + [pltpu.VMEM((7, width, 2 * width), BF)] * 2,
        ),
        out_shape=jax.ShapeDtypeStruct((2, nb + 4, width), F32),
        compiler_params=params(),
        cost_estimate=cost(),
    )(info, x, weights, single, double)


def operators_kernel(ids, freqs, own_band, chip_band, link_bands, one_ref, two_ref, w_ref, vh_ref, vl_ref, top_ref, s_ref, c_ref, *, width, nb, ending):
    wide = 2 * width
    first_slab, last_slab = ids[1] == 0, ids[1] == ids[2] - 1
    row = lax.broadcasted_iota(jnp.int32, (width, width), 0)
    col = lax.broadcasted_iota(jnp.int32, (width, width), 1)
    unit = (row == col).astype(F32)
    taps = []
    for step, ref in enumerate((one_ref, two_ref)):
        complexes = []
        for t in range(3):
            real, imag = ref[0, t * width : (t + 1) * width], ref[1, t * width : (t + 1) * width]
            if step == 0 and ending:
                real = jnp.where(ids[0] < 2, unit if t == 1 else jnp.zeros_like(unit), real)
                imag = jnp.where(ids[0] < 2, jnp.zeros_like(unit), imag)
            if step == 0:
                s_ref[t, 0] = real
                s_ref[t, 1] = imag
            complexes.append((real, imag))
        top = jnp.zeros((1, 1), F32)
        for real, imag in complexes:
            both = jnp.maximum(jnp.abs(real), jnp.abs(imag))
            top = jnp.maximum(top, jnp.max(jnp.max(both, axis=0, keepdims=True), axis=1, keepdims=True))
        top = jnp.where(top > 0, top, 1.0)
        top_ref[step : step + 1] = jnp.broadcast_to(top, (1, width))
        scaled = []
        for t, (real, imag) in enumerate(complexes):
            full = jnp.concatenate(
                [jnp.concatenate([real, imag], axis=1), jnp.concatenate([-imag, real], axis=1)], axis=0
            )
            high, low = split(full)
            for at, value in ((t, high), (3 + t, high), (6 + t, low)):
                w_ref[step, at * wide : (at + 1) * wide] = value
            scaled.append(full / top)
        taps.append(scaled)
    pairs = {
        (a, b): jnp.dot(taps[0][a], taps[1][b], precision=lax.Precision.HIGHEST, preferred_element_type=F32)
        for a in range(3)
        for b in range(3)
    }
    five = [sum(pairs[a, d - a] for a in range(3) if 0 <= d - a < 3) for d in range(5)]
    lost_first = jnp.where(first_slab, pairs[2, 0], 0.0)
    lost_last = jnp.where(last_slab, pairs[0, 2], 0.0)
    first = five[2] - lost_first
    if nb == 1:
        first = first - lost_last
    for number, value in enumerate([*five, first, five[2] - lost_last]):
        high, low = split(value.T)
        vh_ref[number] = high
        vl_ref[number] = low
    for number, value in enumerate([*five, pairs[2, 0], pairs[0, 2]]):
        c_ref[number, 0] = value[:width, :width]
        c_ref[number, 1] = value[:width, width:]


def prepared(ids, freqs, bands, operators, width, nb, ticks, ending):
    rows = operators.shape[3]
    wide = 2 * width

    def chosen(step):
        def index(i, ids, freqs, own_band, chip_band, link_bands):
            k, odd = ids[0], ids[0] % 2 == 1
            if ending:
                freq = freqs[jnp.maximum(ticks + k - 2, ticks - 1)]
                if step == 0:
                    band = link_bands[1]
                else:
                    band = jnp.where(odd, chip_band[0], jnp.where(k == 0, own_band[0], link_bands[0]))
            else:
                freq = freqs[ticks + k]
                band = own_band[0] if step == 0 else jnp.where(odd, link_bands[0], chip_band[0])
            return freq, band, 0, 0, 0

        return pl.BlockSpec((None, None, 2, rows, width), index)

    shapes = [
        ((2, 9 * wide, wide), BF),
        ((7, wide, wide), BF),
        ((7, wide, wide), BF),
        ((2, width), F32),
        ((3, 2, width, width), F32),
        ((7, 2, width, width), F32),
    ]

    def whole(shape):
        return pl.BlockSpec(shape, lambda i, *_: (0,) * len(shape))

    return pl.pallas_call(
        functools.partial(operators_kernel, width=width, nb=nb, ending=ending),
        grid_spec=pltpu.PrefetchScalarGridSpec(
            num_scalar_prefetch=5,
            grid=(1,),
            in_specs=[chosen(0), chosen(1)],
            out_specs=[whole(shape) for shape, _ in shapes],
        ),
        out_shape=[jax.ShapeDtypeStruct(shape, dtype) for shape, dtype in shapes],
        compiler_params=params(),
        cost_estimate=cost(),
    )(ids, freqs, *bands, operators, operators)


def body(state, fresh, operators, band, freq_sched):
    nz, ns = lax.axis_size("depth"), lax.axis_size("slab")
    k, s = lax.axis_index("depth"), lax.axis_index("slab")
    rows, cols = state.shape[2:]
    width = operators.shape[-1]
    ticks = fresh.shape[0]
    nb = rows // width
    paired = ns == 4 and nb == 4
    pb = 2 if paired else nb
    parts = nb // pb
    chunks = 2 if (cols // width) % 4 == 0 else 1
    per = cols // chunks
    is_first, is_last = s == 0, s == ns - 1
    faced = jnp.where(s % 2 == 0, 1, 0) if paired else 0
    firsts = [faced * pb, (1 - faced) * pb] if paired else [0]

    odd = k % 2 == 1
    sends = odd & (k < nz - 2)
    ends = (k == 1) | ((k >= 2) & ~odd)

    def numbers(*values):
        return jnp.stack([jnp.asarray(value).astype(jnp.int32) for value in values])

    end_source = jnp.where(ends, jnp.where(k == 1, 2, 1), 0)
    end_mode = jnp.where(ends, 1, jnp.where(k == 0, 2, 0))
    take_mode = numbers(odd & (k > 1))
    passes = ~odd & (k < nz - 2)

    def flat(pairs, members):
        return [(i * ns + a, i * ns + b) for i in members for a, b in pairs]

    def move(value, pairs, members):
        return lax.ppermute(value, AXES, flat(pairs, members))

    def halos(value, members):
        up_pairs = [(i, i + 1) for i in range(ns - 1)]
        down_pairs = [(i + 1, i) for i in range(ns - 1)]
        if nb == 1:
            far_up = move(value, [(i, i + 2) for i in range(ns - 2)], members)
            far_down = move(value, [(i + 2, i) for i in range(ns - 2)], members)
            near_up = move(value, up_pairs, members)
            near_down = move(value, down_pairs, members)
            return [far_up, near_up, near_down, far_down]
        bottom, top = value[:, -2 * width :], value[:, : 2 * width]
        return [move(bottom, up_pairs, members), move(top, down_pairs, members)]

    facing = [(0, 1), (1, 0), (2, 3), (3, 2)]
    across = [(1, 2), (2, 1)]
    out_way, on_way = [(1, 3), (2, 0)], [(3, 2), (0, 1)]
    if paired:
        halo_places = [6 * faced, 6 * (1 - faced)]
    elif nb == 1:
        halo_places = [0, 1, 3, 4]
    else:
        halo_places = [0, nb + 2]
    part_places = [2 + first for first in firsts]

    senders = [i for i in range(1, nz - 2, 2)]
    enders = [i for i in range(nz) if i == 1 or (i >= 2 and i % 2 == 0)]

    chip_band = lax.ppermute(band, "depth", [(i, i ^ 1) for i in range(nz)])
    links = [(i, i + 1) for i in range(1, nz - 1, 2)]
    links += [(j, i) for i, j in links]
    skip = [(i, i + 2) for i in range(0, nz - 2, 2)]
    raw, pieces = [], []
    link_bands = None
    for p in range(parts):
        mode = after(numbers(jnp.where(passes, 1, jnp.where(sends, 2, 0)), firsts[p]), link_bands if p else chip_band)
        pieces.append(rows_of(mode, state, pb, width, chunks))
        raw.append(lax.ppermute(pieces[p][0], "depth", skip))
        if p == 0:
            link_bands = lax.ppermute(jnp.concatenate([band, after(chip_band, pieces[0][0])]), "depth", links)
    bands = (band, chip_band, link_bands)
    if paired:
        sent_halos = [[move(pieces[0][1], facing, senders), move(pieces[1][1], across, senders)]]
        relayed = [move(value, out_way, senders) for value in pieces[1][2:]]
        near = pieces[0][2:]
        if near:
            near = after(near, sent_halos[0][0])
        for value, relay in zip(near, relayed):
            sent_halos.append([move(value, facing, senders), move(relay, on_way, senders)])
    else:
        sent_halos = [halos(state[0], senders)] * chunks

    ids = numbers(k, s, ns)
    own_w, *own_v, own_single, own_double = prepared(ids, freq_sched, bands, operators, width, nb, ticks, False)
    ids = after(ids, own_w)
    end_w, *end_v, end_single, end_double = prepared(ids, freq_sched, bands, operators, width, nb, ticks, True)

    ended, ended_halos = [], [[] for _ in range(chunks)]

    def end_part(p, done):
        mode = after(numbers(end_source, firsts[p]), done)
        whole = paired and p == 0
        ended.append(receivers(mode, [raw[p], fresh], end_w, pb, width, 1 if whole else chunks))
        for c in range(chunks):
            if not paired:
                ended_halos[c] += halos(ended[p][c], enders)
            elif p == 1 and c == 0:
                ended_halos[c] += [move(ended[1][c], across, enders)]
            elif p == 1:
                ended_halos[c] += [move(move(ended[1][c], out_way, enders), on_way, enders)]
        if whole:
            near_end = move(ended[0][0], facing, enders)
            for c in range(chunks):
                ended_halos[c] += [near_end]
        return ended[p][0]

    done = end_part(0, end_w)

    out = None
    for c in range(chunks):
        mode = after(numbers(sends, 2, *halo_places), done)
        out = shots(mode, [state, *sent_halos[c]], own_v, width, nb, c * per, per, cols, into=out)
        done = out

    start = s * nb
    arrived, swath = [], out[None]
    for p in range(parts):
        mode = after(numbers(sends, p * pb), done)
        done = receivers(mode, [swath], own_w, pb, width, 1)[0]
        arrived.append(lax.ppermute(done, "depth", [(i, i + 2) for i in senders]))
        if p == 0:
            mode = after(numbers(start, True), done)
            given = diagonal(mode, state, own_w, own_single, own_double, width)
            mode = after(numbers(start, k == 0), given)
            given_fresh = diagonal(mode, fresh, end_w, end_single, end_double, width)
            done = given_fresh
        if p + 1 < parts:
            done = end_part(p + 1, done)

    out = None
    last = done
    for c in range(chunks):
        groups = [part[min(c, len(part) - 1)] for part in ended] + ended_halos[c]
        mode = after(numbers(end_mode, *part_places, *halo_places), last)
        out = shots(mode, groups, end_v, width, nb, c * per, per, cols, fresh=fresh, into=out)
        last = arrived[0]
        if c == 0:
            scale = own_v[2][0, 0] * own_v[2][1, 0]
            given = jnp.stack([given[0], given[1] * scale, given_fresh[1] * end_v[2][1, 0]])
            given = after(given, out)
            sums = given[:, 2 : nb + 2]
            for shift in sorted({e // nb for e in (-2, -1, nb, nb + 1)}):
                pairs = [(i, i + shift) for i in range(ns) if 0 <= i + shift < ns]
                low, high = max(-2, shift * nb), min(nb + 2, (shift + 1) * nb)
                got = lax.ppermute(given[:, low + 2 : high + 2], "slab", pairs)
                sums = sums.at[:, low - shift * nb : high - shift * nb].add(got)
            second = lax.ppermute(sums[1], "depth", [(i, i + 1) for i in range(nz - 1)])
    for p, value in enumerate(arrived):
        out = place(take_mode, value, out, p * pb * width)
    image = sums[0] + jnp.where(k == 0, sums[2], after(second, out))
    return out[None], image.reshape(1, rows)


def solution(mesh):
    return jax.shard_map(
        body,
        mesh=mesh,
        in_specs=(
            P("depth", None, "slab", None),
            P(None, None, "slab", None),
            P(),
            P("depth"),
            P(),
        ),
        out_specs=(P("depth", None, "slab", None), P("depth", "slab")),
        check_vma=False,
    )
```

time: 801 us -> 276 us (0.34)
  local copies, waits for them, and re-layouts: 301 us -> 1.69 us
  waiting for transfers between devices: 275 us -> 24.4 us
  Pallas kernels: 0 us -> 175 us
  matrix products: 100 us -> 0 us
  other arithmetic: 49.3 us -> 7.69 us
    ppermute x6 -> x18, waiting for transfers between devices: 275 us -> 24.4 us  [the longest x9 23.1 us: move(): return lax.ppermute(value, AXES, flat(pairs, members))]
    pallas_call x0 -> x16, Pallas kernels: none -> 175 us  [the longest x4 62.3 us: receivers(): pl.pallas_call(functools.partial(receivers_kernel, width=width, nb=nb, gr...]
    unnamed x60 -> x10, local copies, waits for them, and re-layouts: 152 us -> 0.02 us
    dot_general x4 -> x0, matrix products: 100 us -> none  [the longest x2 51.9 us: along_last(): jnp.einsum('abi,ij->abj', triple, combined, precision=lax.Precision.HIGHEST)]
    slice x8 -> x4, local copies, waits for them, and re-layouts: 66.4 us -> 1.04 us  [the longest x1 0.52 us: body(): scale = own_v[2][0, 0] * own_v[2][1, 0]]
    concatenate x6 -> x0, local copies, waits for them, and re-layouts: 31.2 us -> none  [the longest x2 25.5 us: extended_2(): value = jnp.concatenate([before, value, after], axis=dim)]
    another operation x4 -> x1, local copies, waits for them, and re-layouts: 21.9 us -> 0.63 us  [numbers(): return jnp.stack([jnp.asarray(value).astype(jnp.int32) for value in values])]
    pad x2 -> x0, local copies, waits for them, and re-layouts: 16.4 us -> none  [along_last(): padded = jnp.pad(field, ((0, 0), (0, 0), (width, width)))]
  transfers between devices with their start and end apart: 6 -> 18, of which waited for: 6 -> 5; matrix products, arithmetic and copies ran while one was open for 5% -> 3% of each run, Pallas kernels for 0% -> 61%
where the time goes in v1:
time: 276 us; the launch traced here: 273 us
  Pallas kernels  175 us (63%)
  starting transfers between devices  61.5 us (22%)
  waiting for transfers between devices  24.4 us (9%)
  other arithmetic  7.69 us (3%)
    pallas_call x4, Pallas kernels, receivers(): pl.pallas_call(functools.partial(receivers_kernel, width=width, nb=nb, gr...  62.3 us
    pallas_call x4, Pallas kernels, shots(): pl.pallas_call(functools.partial(shots_kernel, width=width, nb=nb, count=...  57.7 us
    ppermute x9, waiting for transfers between devices, move(): return lax.ppermute(value, AXES, flat(pairs, members))  23.1 us
    ppermute x2, starting transfers between devices, body(): got = lax.ppermute(given[:, low + 2:high + 2], 'slab', pairs)  21.6 us
    pallas_call x2, Pallas kernels, diagonal(): pl.pallas_call(functools.partial(diagonal_kernel, width=width, total=tota...  21.6 us
    ppermute x9, starting transfers between devices, move(): return lax.ppermute(value, AXES, flat(pairs, members))  20.7 us
    pallas_call x2, Pallas kernels, rows_of(): pl.pallas_call(rows_kernel, grid_spec=pltpu.PrefetchScalarGridSpec(num_sc...  15.1 us
    pallas_call x2, Pallas kernels, prepared(): pl.pallas_call(functools.partial(operators_kernel, width=width, nb=nb, en...  12.6 us
  transfers between devices with their start and end apart: 18, of which 5 were waited for; matrix products, arithmetic and copies ran while one was open for 3% of the time, Pallas kernels for 61%

profile of v1, /device:TPU:1, one launch (start us, length us, event | category | flops | bytes accessed | tf_op | source)
XLA Modules:
  0.0 272.6 jit_solution(11016693028097718678)
XLA Ops:
  0.6 0.1 collective-permute-start
  0.8 0.6 pad_add_fusion.10.mode
  1.4 0.6 collective-permute-done.chip_band
  1.9 7.5 %shard_map.68 = (f32[2,256,2048]{2,1,0:T(8,128)}, f32[2,256,1024]{2,1,0:T(8,128)}, f32[2,256,1024]{2,1,0:T(8,128)}) custom-call(s32[2]{0:T(128)} %pad_add_fusion.10.mode, f32[1,2,512,2048]{3,2,1,0:T(8,128)} %x_ref.6), custom_call_target="tpu_custom_call" | custom-call | flops 1 | bytes 1 | tf_op jit(solution)/shard_map/pallas_call | solution.py:55
  9.5 2.7 collective-permute-start.2
  12.8 0.7 pad_add_fusion.7.mode
  13.4 0.7 pad_add_fusion.6
  14.1 5.4 %collective-permute-start.1 = (s32[2]{0:T(128)S(1)}, s32[2]{0:T(128)S(1)}, u32[]{:S(2)}, u32[]{:S(2)}) collective-permute-start(s32[2]{0:T(128)S(1)} %pad_add_fusion.6), channel_id=1, source_target_pairs={{4,8},{12,16},{20,24},{8,4},{16,12},{24,20},{5,9},{13,17},{21,25},... | collective-permute-start | bytes 32 | tf_op jit(solution)/shard_map/ppermute | solution.py:507
  19.5 3.1 %collective-permute-start.3 = (f32[2,256,1024]{2,1,0:T(8,128)}, f32[2,256,1024]{2,1,0:T(8,128)}, u32[]{:S(2)}, u32[]{:S(2)}) collective-permute-start(f32[2,256,1024]{2,1,0:T(8,128)} %get-tuple-element.71), channel_id=1, source_target_pairs={{4,5},{5,4},{6,7},{7,6},{12,13},{13,12},{14,15},{15,14},{20,21},{2... | collective-permute-start | bytes 6291464 | tf_op jit(solution)/shard_map/ppermute | solution.py:468
  22.6 0.0 collective-permute-done.1.link_bands
  22.6 7.6 %shard_map.72 = (f32[2,256,2048]{2,1,0:T(8,128)}, f32[2,256,1024]{2,1,0:T(8,128)}, f32[2,256,1024]{2,1,0:T(8,128)}) custom-call(s32[2]{0:T(128)} %pad_add_fusion.7.mode, f32[1,2,512,2048]{3,2,1,0:T(8,128)} %x_ref.6), custom_call_target="tpu_custom_call" | custom-call | flops 1 | bytes 1 | tf_op jit(solution)/shard_map/pallas_call | solution.py:55
  30.2 1.3 collective-permute-start.6
  31.5 2.6 collective-permute-start.8
  34.1 2.0 collective-permute-start.4
  36.1 10.5 %collective-permute-done.3.refs_1_ = f32[2,256,1024]{2,1,0:T(8,128)} collective-permute-done((f32[2,256,1024]{2,1,0:T(8,128)}, f32[2,256,1024]{2,1,0:T(8,128)}, u32[]{:S(2)}, u32[]{:S(2)}) %collective-permute-start.3) | collective-permute-done | bytes 2097184 | tf_op jit(solution)/shard_map/ppermute | solution.py:468
  46.6 3.1 %collective-permute-start.5 = (f32[2,256,1024]{2,1,0:T(8,128)}, f32[2,256,1024]{2,1,0:T(8,128)}, u32[]{:S(2)}, u32[]{:S(2)}) collective-permute-start(f32[2,256,1024]{2,1,0:T(8,128)} %get-tuple-element.79), channel_id=1, source_target_pairs={{4,5},{5,4},{6,7},{7,6},{12,13},{13,12},{14,15},{15,14},{20,21},{2... | collective-permute-start | bytes 6291464 | tf_op jit(solution)/shard_map/ppermute | solution.py:468
  49.7 7.6 %collective-permute-done.6 = f32[2,256,1024]{2,1,0:T(8,128)} collective-permute-done((f32[2,256,1024]{2,1,0:T(8,128)}, f32[2,256,1024]{2,1,0:T(8,128)}, u32[]{:S(2)}, u32[]{:S(2)}) %collective-permute-start.6) | collective-permute-done | bytes 2097184 | tf_op jit(solution)/shard_map/ppermute | solution.py:468
  57.3 2.8 %collective-permute-start.7 = (f32[2,256,1024]{2,1,0:T(8,128)}, f32[2,256,1024]{2,1,0:T(8,128)}, u32[]{:S(2)}, u32[]{:S(2)}) collective-permute-start(f32[2,256,1024]{2,1,0:T(8,128)} %collective-permute-done.6), channel_id=1, source_target_pairs={{7,6},{4,5},{15,14},{12,13},{23,22},{20,21}} | collective-permute-start | bytes 6291464 | tf_op jit(solution)/shard_map/ppermute | solution.py:468
  60.1 0.6 pad_add_fusion.9.mode
  60.7 0.7 pad_add_fusion.5.ids
  61.4 6.3 %shard_map.69 = (bf16[2,2304,256]{2,1,0:T(8,128)(2,1)}, bf16[7,256,256]{2,1,0:T(8,128)(2,1)}, bf16[7,256,256]{2,1,0:T(8,128)(2,1)}, f32[2,128]{1,0:T(2,128)}, f3...) custom-call(s32[3]{0:T(128)} %pad_add_fusion.5.ids, s32[10]{0:T(128)} %freqs.3, s32[1]{0:T(128)S(6)} %copy.17.own_band, ...), custom_call_target="tpu_custom_call" | custom-call | flops 1 | bytes 1 | tf_op jit(solution)/shard_map/pallas_call | solution.py:422
  67.6 6.3 %shard_map.70 = (bf16[2,2304,256]{2,1,0:T(8,128)(2,1)}, bf16[7,256,256]{2,1,0:T(8,128)(2,1)}, bf16[7,256,256]{2,1,0:T(8,128)(2,1)}, f32[2,128]{1,0:T(2,128)}, f3...) custom-call(s32[3]{0:T(128)} %pad_add_fusion.5.ids, s32[10]{0:T(128)} %freqs.3, s32[1]{0:T(128)S(6)} %copy.17.own_band, ...), custom_call_target="tpu_custom_call" | custom-call | flops 1 | bytes 1 | tf_op jit(solution)/shard_map/pallas_call | solution.py:422
  73.9 0.0 collective-permute-done.2.refs_0_
  73.9 15.8 %shard_map.71.refs_0_ = f32[2,256,2048]{2,1,0:T(8,128)} custom-call(s32[2]{0:T(128)} %pad_add_fusion.9.mode, f32[2,256,2048]{2,1,0:T(8,128)} %collective-permute-done.2.refs_0_, f32[2,2,512,2048]{3,2,1,0:T(8,128)} %refs_7_.3, bf16[2,2304,256]{2,1,0:T(8,128)(2,1)} %get-tuple-element.68.refs_2_.w_ref), custom_call_target="tpu_custom_call" | custom-call | flops 1 | bytes 1 | tf_op jit(solution)/shard_map/pallas_call | solution.py:132
  89.7 2.1 collective-permute-start.11
  91.9 0.6 pad_add_fusion.8.mode
  92.5 0.6 pad_add_fusion.3.mode
  93.1 0.7 pad_add_fusion.mode
  93.8 0.7 pad_add_fusion.4.mode
  94.4 0.6 pad_add_fusion.1
  95.1 0.0 collective-permute-done.4.refs_2_
  95.1 14.1 %shard_map.73.refs_6_ = f32[2,512,2048]{2,1,0:T(8,128)} custom-call(s32[4]{0:T(128)} %pad_add_fusion.4.mode, f32[1,2,512,2048]{3,2,1,0:T(8,128)} %x_ref.6, f32[2,256,1024]{2,1,0:T(8,128)} %collective-permute-done.3.refs_1_, f32[2,256,1024]{2,1,0:T(8,128)} %collective-permute-done.4.refs_2_, bf16[7,256,256]{2,1,0:T(8,128)(2,1)} %get-tuple-element.74.refs_3_, ...), custom_call_target="tpu_custom_call" | custom-call | flops 1 | bytes 1 | tf_op jit(solution)/shard_map/pallas_call | solution.py:220
  109.2 0.0 collective-permute-done.5.refs_1_
  109.2 0.0 collective-permute-done.7.refs_2_
  109.2 14.1 %shard_map.74 = f32[2,512,2048]{2,1,0:T(8,128)} custom-call(s32[4]{0:T(128)} %pad_add_fusion.4.mode, f32[1,2,512,2048]{3,2,1,0:T(8,128)} %x_ref.6, f32[2,256,1024]{2,1,0:T(8,128)} %collective-permute-done.5.refs_1_, f32[2,256,1024]{2,1,0:T(8,128)} %collective-permute-done.7.refs_2_, ...), custom_call_target="tpu_custom_call", output_to_operand_aliasing={{}: (7, {})} | custom-call | flops 1 | bytes 1 | tf_op jit(solution)/shard_map/pallas_call | solution.py:220
  123.3 15.3 %shard_map.75 = f32[2,256,2048]{2,1,0:T(8,128)} custom-call(s32[2]{0:T(128)} %pad_add_fusion.3.mode, f32[1,2,512,2048]{3,2,1,0:T(8,128)} %bitcast.32, bf16[2,2304,256]{2,1,0:T(8,128)(2,1)} %get-tuple-element.66.refs_1_.w_ref), custom_call_target="tpu_custom_call" | custom-call | flops 1 | bytes 1 | tf_op jit(solution)/shard_map/pallas_call | solution.py:132
  138.6 3.3 %collective-permute-start.10 = (f32[2,256,2048]{2,1,0:T(8,128)}, f32[2,256,2048]{2,1,0:T(8,128)}, u32[]{:S(2)}, u32[]{:S(2)}) collective-permute-start(f32[2,256,2048]{2,1,0:T(8,128)} %shard_map.75), channel_id=1, source_target_pairs={{4,12},{12,20},{20,28},{5,13},{13,21},{21,29},{6,14},{14,22},{22,3... | collective-permute-start | bytes 12582920 | tf_op jit(solution)/shard_map/ppermute | solution.py:557
  141.8 17.7 %shard_map.76 = f32[2,8,128]{2,1,0:T(8,128)} custom-call(s32[2]{0:T(128)} %get-tuple-element.82.info, f32[1,2,512,2048]{3,2,1,0:T(8,128)} %x_ref.6, bf16[2,2304,256]{2,1,0:T(8,128)(2,1)} %get-tuple-element.66.refs_1_.w_ref, f32[3,2,128,128]{3,2,1,0:T(8,128)} %get-tuple-element.83.s_ref, f32[7,2,128,128]{3,2,1,0:T(8,128)} %get-tuple-element.84.c_ref), custom_call_target="tpu_custom_call" | custom-call | flops 1 | bytes 1 | tf_op jit(solution)/shard_map/pallas_call | solution.py:316
  159.5 3.9 %shard_map.77 = f32[2,8,128]{2,1,0:T(8,128)} custom-call(s32[2]{0:T(128)} %get-tuple-element.85.info, f32[2,2,512,2048]{3,2,1,0:T(8,128)} %refs_7_.3, bf16[2,2304,256]{2,1,0:T(8,128)(2,1)} %get-tuple-element.68.refs_2_.w_ref, f32[3,2,128,128]{3,2,1,0:T(8,128)} %get-tuple-element.86.s_ref, f32[7,2,128,128]{3,2,1,0:T(8,128)} %get-tuple-element.87.c_ref), custom_call_target="tpu_custom_call" | custom-call | flops 1 | bytes 1 | tf_op jit(solution)/shard_map/pallas_call | solution.py:316
  163.4 0.0 collective-permute-done.8.refs_0_
  163.4 15.9 %shard_map.78 = (f32[2,256,1024]{2,1,0:T(8,128)}, f32[2,256,1024]{2,1,0:T(8,128)}) custom-call(s32[2]{0:T(128)} %pad_add_fusion.8.mode, f32[2,256,2048]{2,1,0:T(8,128)} %collective-permute-done.8.refs_0_, f32[2,2,512,2048]{3,2,1,0:T(8,128)} %refs_7_.3, bf16[2,2304,256]{2,1,0:T(8,128)(2,1)} %get-tuple-element.68.refs_2_.w_ref), custom_call_target="tpu_custom_call" | custom-call | flops 1 | bytes 1 | tf_op jit(solution)/shard_map/pallas_call | solution.py:132
  179.3 1.5 collective-permute-start.12
  180.9 0.0 copy-start.2
  180.9 15.3 %shard_map.79 = f32[2,256,2048]{2,1,0:T(8,128)} custom-call(s32[2]{0:T(128)} %pad_add_fusion.mode, f32[1,2,512,2048]{3,2,1,0:T(8,128)} %bitcast.33, bf16[2,2304,256]{2,1,0:T(8,128)(2,1)} %get-tuple-element.66.refs_1_.w_ref), custom_call_target="tpu_custom_call" | custom-call | flops 1 | bytes 1 | tf_op jit(solution)/shard_map/pallas_call | solution.py:132
  196.2 3.2 %collective-permute-start.9 = (f32[2,256,2048]{2,1,0:T(8,128)}, f32[2,256,2048]{2,1,0:T(8,128)}, u32[]{:S(2)}, u32[]{:S(2)}) collective-permute-start(f32[2,256,2048]{2,1,0:T(8,128)} %shard_map.79), channel_id=1, source_target_pairs={{4,12},{12,20},{20,28},{5,13},{13,21},{21,29},{6,14},{14,22},{22,3... | collective-permute-start | bytes 12582920 | tf_op jit(solution)/shard_map/ppermute | solution.py:557
  199.5 2.0 collective-permute-start.14
  201.4 5.0 %collective-permute-done.12 = f32[2,256,1024]{2,1,0:T(8,128)} collective-permute-done((f32[2,256,1024]{2,1,0:T(8,128)}, f32[2,256,1024]{2,1,0:T(8,128)}, u32[]{:S(2)}, u32[]{:S(2)}) %collective-permute-start.12) | collective-permute-done | bytes 2097184 | tf_op jit(solution)/shard_map/ppermute | solution.py:468
  206.4 2.8 %collective-permute-start.13 = (f32[2,256,1024]{2,1,0:T(8,128)}, f32[2,256,1024]{2,1,0:T(8,128)}, u32[]{:S(2)}, u32[]{:S(2)}) collective-permute-start(f32[2,256,1024]{2,1,0:T(8,128)} %collective-permute-done.12), channel_id=1, source_target_pairs={{7,6},{4,5},{11,10},{8,9},{19,18},{16,17},{27,26},{24,25}} | collective-permute-start | bytes 6291464 | tf_op jit(solution)/shard_map/ppermute | solution.py:468
  209.2 0.6 stack.138.mode
  209.9 0.5 slice.90
  210.4 0.5 fusion.5
  212.1 0.7 slice_multiply_fusion
  212.8 0.0 collective-permute-done.14.refs_3_
  212.8 14.7 %shard_map.80.refs_8_ = f32[2,512,2048]{2,1,0:T(8,128)} custom-call(s32[5]{0:T(128)} %stack.138.mode, f32[2,256,2048]{2,1,0:T(8,128)} %shard_map.71.refs_0_, f32[2,256,1024]{2,1,0:T(8,128)} %get-tuple-element.90.refs_1_, f32[2,256,2048]{2,1,0:T(8,128)} %collective-permute-done.11.refs_2_, f32[2,256,1024]{2,1,0:T(8,128)} %collective-permute-done.14.refs_3_, ...), custom_call_target="tpu_custom_call" | custom-call | flops 1 | bytes 1 | tf_op jit(solution)/shard_map/pallas_call | solution.py:220
  227.5 1.3 collective-permute-start.15
  228.9 20.3 %collective-permute-start.16 = (f32[3,2,128]{2,1,0:T(2,128)S(1)}, f32[3,2,128]{2,1,0:T(2,128)S(1)}, u32[]{:S(2)}, u32[]{:S(2)}) collective-permute-start(f32[3,2,128]{2,1,0:T(2,128)S(1)} %get-tuple-element.100), channel_id=1, source_target_pairs={{0,1},{1,2},{2,3},{4,5},{5,6},{6,7},{8,9},{9,10},{10,11},{12,13},{... | collective-permute-start | bytes 9224 | tf_op jit(solution)/shard_map/ppermute | solution.py:582
  249.2 0.7 collective-permute-done.16
  250.0 1.9 collective-permute-start.17
  251.9 0.0 collective-permute-done.10.new_ref
  251.9 14.7 %shard_map.81.old_ref = f32[2,512,2048]{2,1,0:T(8,128)} custom-call(s32[5]{0:T(128)} %stack.138.mode, f32[2,256,2048]{2,1,0:T(8,128)} %shard_map.71.refs_0_, f32[2,256,1024]{2,1,0:T(8,128)} %get-tuple-element.93.refs_1_, f32[2,256,2048]{2,1,0:T(8,128)} %collective-permute-done.11.refs_2_, ...), custom_call_target="tpu_custom_call", output_to_operand_aliasing={{}: (9, {})} | custom-call | flops 1 | bytes 1 | tf_op jit(solution)/shard_map/pallas_call | solution.py:220
  266.6 2.7 shard_map.82.old_ref
  269.3 0.0 collective-permute-done.9.new_ref
  269.3 2.7 shard_map.83
  272.0 0.6 fusion.2
  (20 shorter events, 0.1 us)
Async XLA Ops:
  0.6 1.3 collective-permute-start
  9.5 64.5 %collective-permute-start.2 = (f32[2,256,2048]{2,1,0:T(8,128)}, f32[2,256,2048]{2,1,0:T(8,128)}, u32[]{:S(2)}, u32[]{:S(2)}) collective-permute-start(f32[2,256,2048]{2,1,0:T(8,128)} %get-tuple-element.64), channel_id=1, source_target_pairs={{0,8},{8,16},{16,24},{1,9},{9,17},{17,25},{2,10},{10,18},{18,26},{... | collective-permute-start | bytes 12582920 | tf_op jit(solution)/shard_map/ppermute | solution.py:505
  14.1 8.5 %collective-permute-start.1 = (s32[2]{0:T(128)S(1)}, s32[2]{0:T(128)S(1)}, u32[]{:S(2)}, u32[]{:S(2)}) collective-permute-start(s32[2]{0:T(128)S(1)} %pad_add_fusion.6), channel_id=1, source_target_pairs={{4,8},{12,16},{20,24},{8,4},{16,12},{24,20},{5,9},{13,17},{21,25},... | collective-permute-start | bytes 32 | tf_op jit(solution)/shard_map/ppermute | solution.py:507
  19.5 27.1 %collective-permute-start.3 = (f32[2,256,1024]{2,1,0:T(8,128)}, f32[2,256,1024]{2,1,0:T(8,128)}, u32[]{:S(2)}, u32[]{:S(2)}) collective-permute-start(f32[2,256,1024]{2,1,0:T(8,128)} %get-tuple-element.71), channel_id=1, source_target_pairs={{4,5},{5,4},{6,7},{7,6},{12,13},{13,12},{14,15},{15,14},{20,21},{2... | collective-permute-start | bytes 6291464 | tf_op jit(solution)/shard_map/ppermute | solution.py:468
  22.6 7.6 %copy-start.4 = (s32[2]{0:T(128)}, s32[2]{0:T(128)S(1)}, u32[]{:S(2)}) copy-start(s32[2]{0:T(128)S(1)} %collective-permute-done.1.link_bands) | copy-start | bytes 28
  30.2 27.1 %collective-permute-start.6 = (f32[2,256,1024]{2,1,0:T(8,128)}, f32[2,256,1024]{2,1,0:T(8,128)}, u32[]{:S(2)}, u32[]{:S(2)}) collective-permute-start(f32[2,256,1024]{2,1,0:T(8,128)} %get-tuple-element.80), channel_id=1, source_target_pairs={{5,7},{6,4},{13,15},{14,12},{21,23},{22,20}} | collective-permute-start | bytes 6291464 | tf_op jit(solution)/shard_map/ppermute | solution.py:468
  31.5 131.9 %collective-permute-start.8 = (f32[2,256,2048]{2,1,0:T(8,128)}, f32[2,256,2048]{2,1,0:T(8,128)}, u32[]{:S(2)}, u32[]{:S(2)}) collective-permute-start(f32[2,256,2048]{2,1,0:T(8,128)} %get-tuple-element.89), channel_id=1, source_target_pairs={{0,8},{8,16},{16,24},{1,9},{9,17},{17,25},{2,10},{10,18},{18,26},{... | collective-permute-start | bytes 12582920 | tf_op jit(solution)/shard_map/ppermute | solution.py:505
  34.1 61.0 %collective-permute-start.4 = (f32[2,256,1024]{2,1,0:T(8,128)}, f32[2,256,1024]{2,1,0:T(8,128)}, u32[]{:S(2)}, u32[]{:S(2)}) collective-permute-start(f32[2,256,1024]{2,1,0:T(8,128)} %get-tuple-element.73), channel_id=1, source_target_pairs={{5,6},{6,5},{13,14},{14,13},{21,22},{22,21}} | collective-permute-start | bytes 6291464 | tf_op jit(solution)/shard_map/ppermute | solution.py:468
  46.6 62.6 %collective-permute-start.5 = (f32[2,256,1024]{2,1,0:T(8,128)}, f32[2,256,1024]{2,1,0:T(8,128)}, u32[]{:S(2)}, u32[]{:S(2)}) collective-permute-start(f32[2,256,1024]{2,1,0:T(8,128)} %get-tuple-element.79), channel_id=1, source_target_pairs={{4,5},{5,4},{6,7},{7,6},{12,13},{13,12},{14,15},{15,14},{20,21},{2... | collective-permute-start | bytes 6291464 | tf_op jit(solution)/shard_map/ppermute | solution.py:468
  57.3 51.9 %collective-permute-start.7 = (f32[2,256,1024]{2,1,0:T(8,128)}, f32[2,256,1024]{2,1,0:T(8,128)}, u32[]{:S(2)}, u32[]{:S(2)}) collective-permute-start(f32[2,256,1024]{2,1,0:T(8,128)} %collective-permute-done.6), channel_id=1, source_target_pairs={{7,6},{4,5},{15,14},{12,13},{23,22},{20,21}} | collective-permute-start | bytes 6291464 | tf_op jit(solution)/shard_map/ppermute | solution.py:468
  89.7 123.1 %collective-permute-start.11 = (f32[2,256,2048]{2,1,0:T(8,128)}, f32[2,256,2048]{2,1,0:T(8,128)}, u32[]{:S(2)}, u32[]{:S(2)}) collective-permute-start(f32[2,256,2048]{2,1,0:T(8,128)} %shard_map.71.refs_0_), channel_id=1, source_target_pairs={{4,5},{5,4},{6,7},{7,6},{8,9},{9,8},{10,11},{11,10},{16,17},{17,16... | collective-permute-start | bytes 12582920 | tf_op jit(solution)/shard_map/ppermute | solution.py:468
  138.6 113.3 %collective-permute-start.10 = (f32[2,256,2048]{2,1,0:T(8,128)}, f32[2,256,2048]{2,1,0:T(8,128)}, u32[]{:S(2)}, u32[]{:S(2)}) collective-permute-start(f32[2,256,2048]{2,1,0:T(8,128)} %shard_map.75), channel_id=1, source_target_pairs={{4,12},{12,20},{20,28},{5,13},{13,21},{21,29},{6,14},{14,22},{22,3... | collective-permute-start | bytes 12582920 | tf_op jit(solution)/shard_map/ppermute | solution.py:557
  179.3 27.1 %collective-permute-start.12 = (f32[2,256,1024]{2,1,0:T(8,128)}, f32[2,256,1024]{2,1,0:T(8,128)}, u32[]{:S(2)}, u32[]{:S(2)}) collective-permute-start(f32[2,256,1024]{2,1,0:T(8,128)} %get-tuple-element.93.refs_1_), channel_id=1, source_target_pairs={{5,7},{6,4},{9,11},{10,8},{17,19},{18,16},{25,27},{26,24}} | collective-permute-start | bytes 6291464 | tf_op jit(solution)/shard_map/ppermute | solution.py:468
  180.9 29.0 %copy-start.3 = (f32[2,128]{1,0:T(2,128)S(1)}, f32[2,128]{1,0:T(2,128)}, u32[]{:S(2)}) copy-start(f32[2,128]{1,0:T(2,128)} %get-tuple-element.96.refs_6_) | copy-start | bytes 3076
  180.9 29.5 %copy-start.2 = (f32[2,128]{1,0:T(2,128)S(1)}, f32[2,128]{1,0:T(2,128)}, u32[]{:S(2)}) copy-start(f32[2,128]{1,0:T(2,128)} %get-tuple-element.76.refs_5_) | copy-start | bytes 3076
  180.9 31.2 %copy-start.1 = (f32[2,8,128]{2,1,0:T(8,128)S(1)}, f32[2,8,128]{2,1,0:T(8,128)}, u32[]{:S(2)}) copy-start(f32[2,8,128]{2,1,0:T(8,128)} %shard_map.77) | copy-start | bytes 24580
  180.9 31.9 %copy-start = (f32[2,8,128]{2,1,0:T(8,128)S(1)}, f32[2,8,128]{2,1,0:T(8,128)}, u32[]{:S(2)}) copy-start(f32[2,8,128]{2,1,0:T(8,128)} %shard_map.76) | copy-start | bytes 24580
  196.2 73.1 %collective-permute-start.9 = (f32[2,256,2048]{2,1,0:T(8,128)}, f32[2,256,2048]{2,1,0:T(8,128)}, u32[]{:S(2)}, u32[]{:S(2)}) collective-permute-start(f32[2,256,2048]{2,1,0:T(8,128)} %shard_map.79), channel_id=1, source_target_pairs={{4,12},{12,20},{20,28},{5,13},{13,21},{21,29},{6,14},{14,22},{22,3... | collective-permute-start | bytes 12582920 | tf_op jit(solution)/shard_map/ppermute | solution.py:557
  199.5 13.3 %collective-permute-start.14 = (f32[2,256,1024]{2,1,0:T(8,128)}, f32[2,256,1024]{2,1,0:T(8,128)}, u32[]{:S(2)}, u32[]{:S(2)}) collective-permute-start(f32[2,256,1024]{2,1,0:T(8,128)} %get-tuple-element.90.refs_1_), channel_id=1, source_target_pairs={{5,6},{6,5},{9,10},{10,9},{17,18},{18,17},{25,26},{26,25}} | collective-permute-start | bytes 6291464 | tf_op jit(solution)/shard_map/ppermute | solution.py:468
  206.4 45.5 %collective-permute-start.13 = (f32[2,256,1024]{2,1,0:T(8,128)}, f32[2,256,1024]{2,1,0:T(8,128)}, u32[]{:S(2)}, u32[]{:S(2)}) collective-permute-start(f32[2,256,1024]{2,1,0:T(8,128)} %collective-permute-done.12), channel_id=1, source_target_pairs={{7,6},{4,5},{11,10},{8,9},{19,18},{16,17},{27,26},{24,25}} | collective-permute-start | bytes 6291464 | tf_op jit(solution)/shard_map/ppermute | solution.py:468
  227.5 21.7 %collective-permute-start.15 = (f32[3,2,128]{2,1,0:T(2,128)S(1)}, f32[3,2,128]{2,1,0:T(2,128)S(1)}, u32[]{:S(2)}, u32[]{:S(2)}) collective-permute-start(f32[3,2,128]{2,1,0:T(2,128)S(1)} %get-tuple-element.101), channel_id=1, source_target_pairs={{1,0},{2,1},{3,2},{5,4},{6,5},{7,6},{9,8},{10,9},{11,10},{13,12},{... | collective-permute-start | bytes 9224 | tf_op jit(solution)/shard_map/ppermute | solution.py:582
  228.9 21.1 %collective-permute-start.16 = (f32[3,2,128]{2,1,0:T(2,128)S(1)}, f32[3,2,128]{2,1,0:T(2,128)S(1)}, u32[]{:S(2)}, u32[]{:S(2)}) collective-permute-start(f32[3,2,128]{2,1,0:T(2,128)S(1)} %get-tuple-element.100), channel_id=1, source_target_pairs={{0,1},{1,2},{2,3},{4,5},{5,6},{6,7},{8,9},{9,10},{10,11},{12,13},{... | collective-permute-start | bytes 9224 | tf_op jit(solution)/shard_map/ppermute | solution.py:582
  250.0 22.1 %collective-permute-start.17 = (f32[4,128]{1,0:T(4,128)S(1)}, f32[4,128]{1,0:T(4,128)S(1)}, u32[]{:S(2)}, u32[]{:S(2)}) collective-permute-start(f32[4,128]{1,0:T(4,128)S(1)} %slice_bitcast_fusion), channel_id=1, source_target_pairs={{0,4},{4,8},{8,12},{12,16},{16,20},{20,24},{24,28},{1,5},{5,9},{9,... | collective-permute-start | bytes 6152 | tf_op jit(solution)/shard_map/ppermute | solution.py:584

commit v2 on v1

--- a/solution.py
+++ b/solution.py
@@ -46,7 +46,7 @@
 
 def rows_of(mode, x, blocks, width, chunks):
     cols = x.shape[-1]
-    tall = width // 4
+    tall = width // 2
     lengths = [(1, cols)] + [(2, cols // chunks)] * chunks
 
     def part(wanted, length):
@@ -56,11 +56,11 @@
         rows_kernel,
         grid_spec=pltpu.PrefetchScalarGridSpec(
             num_scalar_prefetch=1,
-            grid=(4 * blocks,),
+            grid=(2 * blocks,),
             in_specs=[
                 pl.BlockSpec(
                     (None, 2, tall, cols),
-                    lambda i, mode: (0, 0, 4 * mode[1] + jnp.where(mode[0] > 0, i, 0), 0),
+                    lambda i, mode: (0, 0, 2 * mode[1] + jnp.where(mode[0] > 0, i, 0), 0),
                 )
             ],
             out_specs=[part(*item) for item in lengths],
@@ -117,26 +117,28 @@
 def receivers(mode, sources, weights, blocks, width, chunks):
     cols = sources[0].shape[-1]
     nb = cols // width
-    group = 2 if nb % 2 == 0 else 1
+    group = 4 if nb % 4 == 0 else 1
+    tall = width // 2
+    steps = blocks * (width // tall)
     per = cols // chunks
     in_specs = []
     for number, array in enumerate(sources):
         lead = (None,) * (array.ndim - 3)
 
         def rows_at(i, mode, number=number, lead=lead):
-            first = mode[1] if lead else 0
+            first = mode[1] * (width // tall) if lead else 0
             return (0,) * len(lead) + (0, first + jnp.where(mode[0] == number + 1, i, 0), 0)
 
-        in_specs.append(pl.BlockSpec((*lead, 2, width, cols), rows_at))
+        in_specs.append(pl.BlockSpec((*lead, 2, tall, cols), rows_at))
     in_specs.append(pl.BlockSpec(weights.shape, lambda i, mode: (0, 0, 0)))
     return pl.pallas_call(
         functools.partial(receivers_kernel, width=width, nb=nb, group=group, sources=len(sources), chunks=chunks),
         grid_spec=pltpu.PrefetchScalarGridSpec(
             num_scalar_prefetch=1,
-            grid=(blocks,),
+            grid=(steps,),
             in_specs=in_specs,
-            out_specs=[pl.BlockSpec((2, width, per), lambda i, mode: (0, jnp.where(mode[0] > 0, i, 0), 0))] * chunks,
-            scratch_shapes=[pltpu.VMEM((nb + 2, width, 2 * width), BF)] * 4,
+            out_specs=[pl.BlockSpec((2, tall, per), lambda i, mode: (0, jnp.where(mode[0] > 0, i, 0), 0))] * chunks,
+            scratch_shapes=[pltpu.VMEM((nb + 2, tall, 2 * width), BF)] * 4,
         ),
         out_shape=[jax.ShapeDtypeStruct((2, blocks * width, per), F32)] * chunks,
         compiler_params=params(),
@@ -168,21 +170,26 @@
 def shots_kernel(mode, *refs, width, nb, count, fresh):
     groups, rest = refs[:count], refs[count:]
     vh_ref, vl_ref, top_ref = rest[:3]
-    o_ref, xh, xl = rest[-3:]
-
-    def store(b, y):
-        y = y * top_ref[0:1, 0:1] * top_ref[1:2, 0:1]
-        for p in range(2):
-            o_ref[p, b * width : (b + 1) * width] = y[p * width : (p + 1) * width]
+    xh, xl = rest[-2:]
+    o_ref, q_ref = (rest[-4], rest[-3]) if fresh else (rest[-3], None)
+
+    def run(ref):
+        def store(b, y):
+            y = y * top_ref[0:1, 0:1] * top_ref[1:2, 0:1]
+            for p in range(2):
+                ref[p, b * width : (b + 1) * width] = y[p * width : (p + 1) * width]
+
+        shots_body(mode, groups, vh_ref, vl_ref, xh, xl, store, width, nb)
 
     @pl.when(mode[0] == 1)
     def _():
-        shots_body(mode, groups, vh_ref, vl_ref, xh, xl, store, width, nb)
+        run(o_ref)
 
     if fresh:
 
         @pl.when(mode[0] == 2)
         def _():
+            run(q_ref)
             o_ref[...] = rest[3][...]
 
 
@@ -197,7 +204,7 @@
         lead = (None,) * (array.ndim - 3)
         return pl.BlockSpec(
             (*lead, 2, array.shape[-2], ct),
-            lambda i, mode: (0,) * (len(lead) + 2) + (first + jnp.where(mode[0] == 1, i, 0),),
+            lambda i, mode: (0,) * (len(lead) + 2) + (first + jnp.where(mode[0] > 0, i, 0),),
         )
 
     in_specs = [columns(array) for array in groups]
@@ -205,7 +212,11 @@
     in_specs.append(pl.BlockSpec(tops.shape, lambda i, mode: (0, 0)))
     operands = [*groups, vh, vl, tops]
     aliases = {}
+    out_specs = [pl.BlockSpec((2, rows, ct), lambda i, mode: (0, 0, start + jnp.where(mode[0] > 0, i, 0)))]
+    out_shape = [jax.ShapeDtypeStruct((2, rows, total), F32)]
     if fresh is not None:
+        out_specs.append(pl.BlockSpec((2, rows, ct), lambda i, mode: (0, 0, jnp.where(mode[0] == 2, i, 0))))
+        out_shape.append(jax.ShapeDtypeStruct((2, rows, length), F32))
         in_specs.append(
             pl.BlockSpec(
                 (None, 2, rows, ct),
@@ -223,10 +234,10 @@
             num_scalar_prefetch=1,
             grid=(length // ct,),
             in_specs=in_specs,
-            out_specs=pl.BlockSpec((2, rows, ct), lambda i, mode: (0, 0, start + jnp.where(mode[0] > 0, i, 0))),
+            out_specs=out_specs,
             scratch_shapes=[pltpu.VMEM(((nb + 4) * 2 * width, ct), BF)] * 2,
         ),
-        out_shape=jax.ShapeDtypeStruct((2, rows, total), F32),
+        out_shape=out_shape,
         input_output_aliases=aliases,
         compiler_params=params(),
         cost_estimate=cost(),
@@ -243,10 +254,10 @@
         o_ref[...] = old_ref[...]
 
 
-def place(mode, new, into, at):
+def place(mode, new, into, row, col):
     rows, cols = new.shape[1:]
-    tall = math.gcd(rows, 32)
-    start = at // tall
+    tall = math.gcd(math.gcd(rows, row), max(8, (1 << 17) // cols))
+    start, across = row // tall, col // cols
     return pl.pallas_call(
         place_kernel,
         grid_spec=pltpu.PrefetchScalarGridSpec(
@@ -254,9 +265,11 @@
             grid=(rows // tall,),
             in_specs=[
                 pl.BlockSpec((2, tall, cols), lambda i, mode: (0, jnp.where(mode[0] == 1, i, 0), 0)),
-                pl.BlockSpec((2, tall, cols), lambda i, mode: (0, start, 0)),
+                pl.BlockSpec((2, tall, cols), lambda i, mode: (0, start, across)),
             ],
-            out_specs=pl.BlockSpec((2, tall, cols), lambda i, mode: (0, start + jnp.where(mode[0] == 1, i, 0), 0)),
+            out_specs=pl.BlockSpec(
+                (2, tall, cols), lambda i, mode: (0, start + jnp.where(mode[0] == 1, i, 0), across)
+            ),
         ),
         out_shape=jax.ShapeDtypeStruct(into.shape, F32),
         input_output_aliases={2: 0},
@@ -451,13 +464,13 @@
 
     odd = k % 2 == 1
     sends = odd & (k < nz - 2)
-    ends = (k == 1) | ((k >= 2) & ~odd)
+    ends = ~odd
 
     def numbers(*values):
         return jnp.stack([jnp.asarray(value).astype(jnp.int32) for value in values])
 
-    end_source = jnp.where(ends, jnp.where(k == 1, 2, 1), 0)
-    end_mode = jnp.where(ends, 1, jnp.where(k == 0, 2, 0))
+    end_source = jnp.where(ends, jnp.where(k == 0, 2, 1), 0)
+    end_mode = jnp.where(ends, jnp.where(k == 0, 2, 1), 0)
     take_mode = numbers(odd & (k > 1))
     passes = ~odd & (k < nz - 2)
 
@@ -491,7 +504,7 @@
     part_places = [2 + first for first in firsts]
 
     senders = [i for i in range(1, nz - 2, 2)]
-    enders = [i for i in range(nz) if i == 1 or (i >= 2 and i % 2 == 0)]
+    enders = [i for i in range(0, nz, 2)]
 
     chip_band = lax.ppermute(band, "depth", [(i, i ^ 1) for i in range(nz)])
     links = [(i, i + 1) for i in range(1, nz - 1, 2)]
@@ -522,68 +535,67 @@
     ids = after(ids, own_w)
     end_w, *end_v, end_single, end_double = prepared(ids, freq_sched, bands, operators, width, nb, ticks, True)
 
-    ended, ended_halos = [], [[] for _ in range(chunks)]
-
-    def end_part(p, done):
-        mode = after(numbers(end_source, firsts[p]), done)
-        whole = paired and p == 0
-        ended.append(receivers(mode, [raw[p], fresh], end_w, pb, width, 1 if whole else chunks))
-        for c in range(chunks):
-            if not paired:
-                ended_halos[c] += halos(ended[p][c], enders)
-            elif p == 1 and c == 0:
-                ended_halos[c] += [move(ended[1][c], across, enders)]
-            elif p == 1:
-                ended_halos[c] += [move(move(ended[1][c], out_way, enders), on_way, enders)]
-        if whole:
-            near_end = move(ended[0][0], facing, enders)
-            for c in range(chunks):
-                ended_halos[c] += [near_end]
-        return ended[p][0]
-
-    done = end_part(0, end_w)
+    start = s * nb
+    mode = after(numbers(start, k == 0), end_w)
+    given_fresh = diagonal(mode, fresh, end_w, end_single, end_double, width)
+
+    def end_part(p, *done):
+        mode = after(numbers(end_source, firsts[p]), *done)
+        return receivers(mode, [raw[p], fresh], end_w, pb, width, 1 if paired and p == 0 else chunks)
+
+    ended = [end_part(0, given_fresh)]
+    done = ended[0][0]
 
     out = None
     for c in range(chunks):
         mode = after(numbers(sends, 2, *halo_places), done)
-        out = shots(mode, [state, *sent_halos[c]], own_v, width, nb, c * per, per, cols, into=out)
+        (out,) = shots(mode, [state, *sent_halos[c]], own_v, width, nb, c * per, per, cols, into=out)
         done = out
-
-    start = s * nb
-    arrived, swath = [], out[None]
-    for p in range(parts):
-        mode = after(numbers(sends, p * pb), done)
-        done = receivers(mode, [swath], own_w, pb, width, 1)[0]
-        arrived.append(lax.ppermute(done, "depth", [(i, i + 2) for i in senders]))
-        if p == 0:
-            mode = after(numbers(start, True), done)
-            given = diagonal(mode, state, own_w, own_single, own_double, width)
-            mode = after(numbers(start, k == 0), given)
-            given_fresh = diagonal(mode, fresh, end_w, end_single, end_double, width)
-            done = given_fresh
-        if p + 1 < parts:
-            done = end_part(p + 1, done)
-
-    out = None
-    last = done
+    arrived, at = [], 0
+    for count in [1, nb - 1] if nb > 1 else [nb]:
+        value = receivers(after(numbers(sends, at), done), [out[None]], own_w, count, width, 1)[0]
+        arrived.append((at, lax.ppermute(value, "depth", [(i, i + 2) for i in senders])))
+        done = value
+        if at == 0 and paired:
+            near_end = move(after(ended[0][0], done), facing, enders)
+        at += count
+
+    ended_halos = [[] for _ in range(chunks)]
+    if paired:
+        ended.append(end_part(1, done, arrived[0][1]))
+        done = ended[1][0]
+        for c in range(chunks):
+            value = ended[1][c]
+            crossed = move(value, across, enders) if c == 0 else move(move(value, out_way, enders), on_way, enders)
+            ended_halos[c] = [near_end, crossed]
+    else:
+        ended_halos = [halos(value, enders) for value in ended[0]]
+
+    given = diagonal(after(numbers(start, True), done), state, own_w, own_single, own_double, width)
+
+    out, last, crossing = None, given, []
     for c in range(chunks):
         groups = [part[min(c, len(part) - 1)] for part in ended] + ended_halos[c]
         mode = after(numbers(end_mode, *part_places, *halo_places), last)
-        out = shots(mode, groups, end_v, width, nb, c * per, per, cols, fresh=fresh, into=out)
-        last = arrived[0]
-        if c == 0:
-            scale = own_v[2][0, 0] * own_v[2][1, 0]
-            given = jnp.stack([given[0], given[1] * scale, given_fresh[1] * end_v[2][1, 0]])
-            given = after(given, out)
-            sums = given[:, 2 : nb + 2]
-            for shift in sorted({e // nb for e in (-2, -1, nb, nb + 1)}):
-                pairs = [(i, i + shift) for i in range(ns) if 0 <= i + shift < ns]
-                low, high = max(-2, shift * nb), min(nb + 2, (shift + 1) * nb)
-                got = lax.ppermute(given[:, low + 2 : high + 2], "slab", pairs)
-                sums = sums.at[:, low - shift * nb : high - shift * nb].add(got)
-            second = lax.ppermute(sums[1], "depth", [(i, i + 1) for i in range(nz - 1)])
-    for p, value in enumerate(arrived):
-        out = place(take_mode, value, out, p * pb * width)
+        out, ready = shots(mode, groups, end_v, width, nb, c * per, per, cols, fresh=fresh, into=out)
+        crossing.append(lax.ppermute(ready, "depth", [(0, 1)]))
+        last = arrived[0][1]
+
+    scale = own_v[2][0, 0] * own_v[2][1, 0]
+    given = jnp.stack([given[0], given[1] * scale, given_fresh[1] * end_v[2][1, 0]])
+    given = after(given, out)
+    sums = given[:, 2 : nb + 2]
+    for shift in sorted({e // nb for e in (-2, -1, nb, nb + 1)}):
+        pairs = [(i, i + shift) for i in range(ns) if 0 <= i + shift < ns]
+        low, high = max(-2, shift * nb), min(nb + 2, (shift + 1) * nb)
+        got = lax.ppermute(given[:, low + 2 : high + 2], "slab", pairs)
+        sums = sums.at[:, low - shift * nb : high - shift * nb].add(got)
+    second = lax.ppermute(sums[1], "depth", [(i, i + 1) for i in range(nz - 1)])
+
+    for c, value in enumerate(crossing):
+        out = place(numbers(k == 1), value, out, 0, c * per)
+    for at, value in arrived:
+        out = place(take_mode, value, out, at * width, 0)
     image = sums[0] + jnp.where(k == 0, sums[2], after(second, out))
     return out[None], image.reshape(1, rows)
 

time: 276 us -> 243 us (0.88)
  Pallas kernels: 175 us -> 138 us
  starting transfers between devices: 61.5 us -> 70 us
  waiting for transfers between devices: 24.4 us -> 21.4 us
    pallas_call x4, Pallas kernels: 62.3 us -> 38.2 us  [receivers(): pl.pallas_call(functools.partial(receivers_kernel, width=width, nb=nb, gr...]
    ppermute x1, starting transfers between devices: 1.91 us -> 22.2 us  [body(): second = lax.ppermute(sums[1], 'depth', [(i, i + 1) for i in range(nz - 1)])]
    pallas_call x4, Pallas kernels: 57.7 us -> 37.7 us  [shots(): pl.pallas_call(functools.partial(shots_kernel, width=width, nb=nb, count=...]
    ppermute x2, starting transfers between devices: 21.6 us -> 5.28 us  [body(): got = lax.ppermute(given[:, low + 2:high + 2], 'slab', pairs)]
    pallas_call x2 -> x4, Pallas kernels: 5.36 us -> 16.1 us  [place(): pl.pallas_call(place_kernel, grid_spec=pltpu.PrefetchScalarGridSpec(num_s...]
    ppermute x2 -> x4, starting transfers between devices: 6.49 us -> 10.9 us  [the longest x2 8.32 us: body(): lax.ppermute(value, 'depth', [(i, i + 2) for i in senders])]
    pallas_call x2, Pallas kernels: 15.1 us -> 11.6 us  [rows_of(): pl.pallas_call(rows_kernel, grid_spec=pltpu.PrefetchScalarGridSpec(num_sc...]
  transfers between devices with their start and end apart: 18 -> 20, of which waited for: 5 -> 3; matrix products, arithmetic and copies ran while one was open for 3% -> 4% of each run, Pallas kernels for 61% -> 55%
where the time goes in v2:
time: 243 us; the launch traced here: 242 us
  Pallas kernels  138 us (57%)
  starting transfers between devices  70 us (29%)
  waiting for transfers between devices  21.4 us (9%)
  other arithmetic  7.39 us (3%)
  between operations  2.76 us (1%)
    pallas_call x4, Pallas kernels, receivers(): pl.pallas_call(functools.partial(receivers_kernel, width=width, nb=nb, gr...  38.2 us
    pallas_call x4, Pallas kernels, shots(): pl.pallas_call(functools.partial(shots_kernel, width=width, nb=nb, count=...  37.7 us
    ppermute x1, starting transfers between devices, body(): second = lax.ppermute(sums[1], 'depth', [(i, i + 1) for i in range(nz - 1)])  22.2 us
    pallas_call x2, Pallas kernels, diagonal(): pl.pallas_call(functools.partial(diagonal_kernel, width=width, total=tota...  21.8 us
    ppermute x9, starting transfers between devices, move(): return lax.ppermute(value, AXES, flat(pairs, members))  20.8 us
    ppermute x9, waiting for transfers between devices, move(): return lax.ppermute(value, AXES, flat(pairs, members))  20.7 us
    pallas_call x4, Pallas kernels, place(): pl.pallas_call(place_kernel, grid_spec=pltpu.PrefetchScalarGridSpec(num_s...  16.1 us
    pallas_call x2, Pallas kernels, prepared(): pl.pallas_call(functools.partial(operators_kernel, width=width, nb=nb, en...  12.8 us
  transfers between devices with their start and end apart: 20, of which 3 were waited for; matrix products, arithmetic and copies ran while one was open for 4% of the time, Pallas kernels for 55%

profile of v2, /device:TPU:1, one launch (start us, length us, event | category | flops | bytes accessed | tf_op | source)
XLA Modules:
  0.0 241.5 jit_solution(4242415208239682979)
XLA Ops:
  0.6 0.1 collective-permute-start
  1.4 0.6 pad_add_fusion.10.mode
  2.1 0.6 pad_add_fusion.7.mode
  2.6 0.0 collective-permute-done.chip_band
  2.6 5.8 %shard_map.68 = (f32[2,256,2048]{2,1,0:T(8,128)}, f32[2,256,1024]{2,1,0:T(8,128)}, f32[2,256,1024]{2,1,0:T(8,128)}) custom-call(s32[2]{0:T(128)} %pad_add_fusion.7.mode, f32[1,2,512,2048]{3,2,1,0:T(8,128)} %x_ref.7), custom_call_target="tpu_custom_call" | custom-call | flops 1 | bytes 1 | tf_op jit(solution)/shard_map/pallas_call | solution.py:55
  8.4 2.6 %collective-permute-start.2 = (f32[2,256,2048]{2,1,0:T(8,128)}, f32[2,256,2048]{2,1,0:T(8,128)}, u32[]{:S(2)}, u32[]{:S(2)}) collective-permute-start(f32[2,256,2048]{2,1,0:T(8,128)} %get-tuple-element.69), channel_id=1, source_target_pairs={{0,8},{8,16},{16,24},{1,9},{9,17},{17,25},{2,10},{10,18},{18,26},{... | collective-permute-start | bytes 12582920 | tf_op jit(solution)/shard_map/ppermute | solution.py:518
  11.1 0.7 pad_add_fusion.6
  11.8 5.4 %collective-permute-start.1 = (s32[2]{0:T(128)S(1)}, s32[2]{0:T(128)S(1)}, u32[]{:S(2)}, u32[]{:S(2)}) collective-permute-start(s32[2]{0:T(128)S(1)} %pad_add_fusion.6), channel_id=1, source_target_pairs={{4,8},{12,16},{20,24},{8,4},{16,12},{24,20},{5,9},{13,17},{21,25},... | collective-permute-start | bytes 32 | tf_op jit(solution)/shard_map/ppermute | solution.py:520
  17.2 3.1 %collective-permute-start.3 = (f32[2,256,1024]{2,1,0:T(8,128)}, f32[2,256,1024]{2,1,0:T(8,128)}, u32[]{:S(2)}, u32[]{:S(2)}) collective-permute-start(f32[2,256,1024]{2,1,0:T(8,128)} %get-tuple-element.79), channel_id=1, source_target_pairs={{4,5},{5,4},{6,7},{7,6},{12,13},{13,12},{14,15},{15,14},{20,21},{2... | collective-permute-start | bytes 6291464 | tf_op jit(solution)/shard_map/ppermute | solution.py:481
  20.4 0.0 collective-permute-done.1.link_bands
  20.4 5.8 %shard_map.73 = (f32[2,256,2048]{2,1,0:T(8,128)}, f32[2,256,1024]{2,1,0:T(8,128)}, f32[2,256,1024]{2,1,0:T(8,128)}) custom-call(s32[2]{0:T(128)} %pad_add_fusion.10.mode, f32[1,2,512,2048]{3,2,1,0:T(8,128)} %x_ref.7), custom_call_target="tpu_custom_call" | custom-call | flops 1 | bytes 1 | tf_op jit(solution)/shard_map/pallas_call | solution.py:55
  26.1 1.3 collective-permute-start.6
  27.4 2.0 collective-permute-start.4
  29.4 14.9 %collective-permute-done.3.refs_1_ = f32[2,256,1024]{2,1,0:T(8,128)} collective-permute-done((f32[2,256,1024]{2,1,0:T(8,128)}, f32[2,256,1024]{2,1,0:T(8,128)}, u32[]{:S(2)}, u32[]{:S(2)}) %collective-permute-start.3) | collective-permute-done | bytes 2097184 | tf_op jit(solution)/shard_map/ppermute | solution.py:481
  44.3 3.1 %collective-permute-start.5 = (f32[2,256,1024]{2,1,0:T(8,128)}, f32[2,256,1024]{2,1,0:T(8,128)}, u32[]{:S(2)}, u32[]{:S(2)}) collective-permute-start(f32[2,256,1024]{2,1,0:T(8,128)} %get-tuple-element.87), channel_id=1, source_target_pairs={{4,5},{5,4},{6,7},{7,6},{12,13},{13,12},{14,15},{15,14},{20,21},{2... | collective-permute-start | bytes 6291464 | tf_op jit(solution)/shard_map/ppermute | solution.py:481
  47.4 5.8 %collective-permute-done.6 = f32[2,256,1024]{2,1,0:T(8,128)} collective-permute-done((f32[2,256,1024]{2,1,0:T(8,128)}, f32[2,256,1024]{2,1,0:T(8,128)}, u32[]{:S(2)}, u32[]{:S(2)}) %collective-permute-start.6) | collective-permute-done | bytes 2097184 | tf_op jit(solution)/shard_map/ppermute | solution.py:481
  53.2 2.8 %collective-permute-start.7 = (f32[2,256,1024]{2,1,0:T(8,128)}, f32[2,256,1024]{2,1,0:T(8,128)}, u32[]{:S(2)}, u32[]{:S(2)}) collective-permute-start(f32[2,256,1024]{2,1,0:T(8,128)} %collective-permute-done.6), channel_id=1, source_target_pairs={{7,6},{4,5},{15,14},{12,13},{23,22},{20,21}} | collective-permute-start | bytes 6291464 | tf_op jit(solution)/shard_map/ppermute | solution.py:481
  56.0 2.7 %collective-permute-start.10 = (f32[2,256,2048]{2,1,0:T(8,128)}, f32[2,256,2048]{2,1,0:T(8,128)}, u32[]{:S(2)}, u32[]{:S(2)}) collective-permute-start(f32[2,256,2048]{2,1,0:T(8,128)} %get-tuple-element.93), channel_id=1, source_target_pairs={{0,8},{8,16},{16,24},{1,9},{9,17},{17,25},{2,10},{10,18},{18,26},{... | collective-permute-start | bytes 12582920 | tf_op jit(solution)/shard_map/ppermute | solution.py:518
  58.7 0.6 pad_add_fusion.4.info
  59.3 0.6 pad_add_fusion.2.mode
  59.9 0.6 pad_add_fusion.3.mode
  60.5 0.6 pad_add_fusion.5.ids
  61.1 0.6 pad_add_fusion.1
  61.7 6.4 %shard_map.69 = (bf16[2,2304,256]{2,1,0:T(8,128)(2,1)}, bf16[7,256,256]{2,1,0:T(8,128)(2,1)}, bf16[7,256,256]{2,1,0:T(8,128)(2,1)}, f32[2,128]{1,0:T(2,128)}, f3...) custom-call(s32[3]{0:T(128)} %pad_add_fusion.5.ids, s32[10]{0:T(128)} %freqs.3, s32[1]{0:T(128)S(6)} %copy.21.own_band, ...), custom_call_target="tpu_custom_call" | custom-call | flops 1 | bytes 1 | tf_op jit(solution)/shard_map/pallas_call | solution.py:435
  68.1 6.4 %shard_map.70 = (bf16[2,2304,256]{2,1,0:T(8,128)(2,1)}, bf16[7,256,256]{2,1,0:T(8,128)(2,1)}, bf16[7,256,256]{2,1,0:T(8,128)(2,1)}, f32[2,128]{1,0:T(2,128)}, f3...) custom-call(s32[3]{0:T(128)} %pad_add_fusion.5.ids, s32[10]{0:T(128)} %freqs.3, s32[1]{0:T(128)S(6)} %copy.21.own_band, ...), custom_call_target="tpu_custom_call" | custom-call | flops 1 | bytes 1 | tf_op jit(solution)/shard_map/pallas_call | solution.py:435
  74.5 4.1 %shard_map.71 = f32[2,8,128]{2,1,0:T(8,128)} custom-call(s32[2]{0:T(128)} %pad_add_fusion.4.info, f32[2,2,512,2048]{3,2,1,0:T(8,128)} %refs_7_.3, bf16[2,2304,256]{2,1,0:T(8,128)(2,1)} %get-tuple-element.73.w_ref.refs_2_, f32[3,2,128,128]{3,2,1,0:T(8,128)} %get-tuple-element.75.s_ref, f32[7,2,128,128]{3,2,1,0:T(8,128)} %get-tuple-element.76.c_ref), custom_call_target="tpu_custom_call" | custom-call | flops 1 | bytes 1 | tf_op jit(solution)/shard_map/pallas_call | solution.py:329
  78.6 0.0 collective-permute-done.2.refs_0_
  78.6 4.0 %shard_map.72.refs_0_ = f32[2,256,2048]{2,1,0:T(8,128)} custom-call(s32[2]{0:T(128)} %get-tuple-element.77.mode, f32[2,256,2048]{2,1,0:T(8,128)} %collective-permute-done.2.refs_0_, f32[2,2,512,2048]{3,2,1,0:T(8,128)} %refs_7_.3, bf16[2,2304,256]{2,1,0:T(8,128)(2,1)} %get-tuple-element.73.w_ref.refs_2_), custom_call_target="tpu_custom_call" | custom-call | flops 1 | bytes 1 | tf_op jit(solution)/shard_map/pallas_call | solution.py:134
  82.6 0.0 collective-permute-done.4.refs_2_
  82.6 14.1 %shard_map.74.refs_6_ = f32[2,512,2048]{2,1,0:T(8,128)} custom-call(s32[4]{0:T(128)} %pad_add_fusion.3.mode, f32[1,2,512,2048]{3,2,1,0:T(8,128)} %x_ref.7, f32[2,256,1024]{2,1,0:T(8,128)} %collective-permute-done.3.refs_1_, f32[2,256,1024]{2,1,0:T(8,128)} %collective-permute-done.4.refs_2_, bf16[7,256,256]{2,1,0:T(8,128)(2,1)} %get-tuple-element.82.refs_3_, ...), custom_call_target="tpu_custom_call" | custom-call | flops 1 | bytes 1 | tf_op jit(solution)/shard_map/pallas_call | solution.py:231
  96.7 14.1 %shard_map.75 = f32[2,512,2048]{2,1,0:T(8,128)} custom-call(s32[4]{0:T(128)} %pad_add_fusion.3.mode, f32[1,2,512,2048]{3,2,1,0:T(8,128)} %x_ref.7, f32[2,256,1024]{2,1,0:T(8,128)} %collective-permute-done.5.refs_1_, f32[2,256,1024]{2,1,0:T(8,128)} %collective-permute-done.7.refs_2_, ...), custom_call_target="tpu_custom_call", output_to_operand_aliasing={{}: (7, {})} | custom-call | flops 1 | bytes 1 | tf_op jit(solution)/shard_map/pallas_call | solution.py:231
  110.8 9.3 %shard_map.76 = f32[2,128,2048]{2,1,0:T(8,128)} custom-call(s32[2]{0:T(128)} %pad_add_fusion.2.mode, f32[1,2,512,2048]{3,2,1,0:T(8,128)} %bitcast.33, bf16[2,2304,256]{2,1,0:T(8,128)(2,1)} %get-tuple-element.71.refs_1_.w_ref), custom_call_target="tpu_custom_call" | custom-call | flops 1 | bytes 1 | tf_op jit(solution)/shard_map/pallas_call | solution.py:134
  120.1 3.6 %collective-permute-start.9 = (f32[2,128,2048]{2,1,0:T(8,128)}, f32[2,128,2048]{2,1,0:T(8,128)}, u32[]{:S(2)}, u32[]{:S(2)}) collective-permute-start(f32[2,128,2048]{2,1,0:T(8,128)} %shard_map.76), channel_id=1, source_target_pairs={{4,12},{12,20},{20,28},{5,13},{13,21},{21,29},{6,14},{14,22},{22,3... | collective-permute-start | bytes 6291464 | tf_op jit(solution)/shard_map/ppermute | solution.py:557
  123.7 0.7 pad_add_fusion.9.mode
  124.4 20.6 %shard_map.77 = f32[2,384,2048]{2,1,0:T(8,128)} custom-call(s32[2]{0:T(128)} %get-tuple-element.90.mode, f32[1,2,512,2048]{3,2,1,0:T(8,128)} %bitcast.34, bf16[2,2304,256]{2,1,0:T(8,128)(2,1)} %get-tuple-element.71.refs_1_.w_ref), custom_call_target="tpu_custom_call" | custom-call | flops 1 | bytes 1 | tf_op jit(solution)/shard_map/pallas_call | solution.py:134
  145.0 2.7 %collective-permute-start.11 = (f32[2,256,2048]{2,1,0:T(8,128)}, f32[2,256,2048]{2,1,0:T(8,128)}, u32[]{:S(2)}, u32[]{:S(2)}) collective-permute-start(f32[2,256,2048]{2,1,0:T(8,128)} %shard_map.72.refs_0_), channel_id=1, source_target_pairs={{0,1},{1,0},{2,3},{3,2},{8,9},{9,8},{10,11},{11,10},{16,17},{17,16... | collective-permute-start | bytes 12582920 | tf_op jit(solution)/shard_map/ppermute | solution.py:481
  147.6 0.0 collective-permute-done.9.new_ref
  147.6 4.2 %shard_map.78 = (f32[2,256,1024]{2,1,0:T(8,128)}, f32[2,256,1024]{2,1,0:T(8,128)}) custom-call(s32[2]{0:T(128)} %pad_add_fusion.9.mode, f32[2,256,2048]{2,1,0:T(8,128)} %collective-permute-done.10.refs_0_, f32[2,2,512,2048]{3,2,1,0:T(8,128)} %refs_7_.3, bf16[2,2304,256]{2,1,0:T(8,128)(2,1)} %get-tuple-element.73.w_ref.refs_2_), custom_call_target="tpu_custom_call" | custom-call | flops 1 | bytes 1 | tf_op jit(solution)/shard_map/pallas_call | solution.py:134
  151.9 2.0 collective-permute-start.12
  153.8 2.0 collective-permute-start.14
  155.8 0.0 collective-permute-done.12
  155.8 2.0 collective-permute-start.13
  157.8 4.7 %collective-permute-start.8 = (f32[2,384,2048]{2,1,0:T(8,128)}, f32[2,384,2048]{2,1,0:T(8,128)}, u32[]{:S(2)}, u32[]{:S(2)}) collective-permute-start(f32[2,384,2048]{2,1,0:T(8,128)} %shard_map.77), channel_id=1, source_target_pairs={{4,12},{12,20},{20,28},{5,13},{13,21},{21,29},{6,14},{14,22},{22,3... | collective-permute-start | bytes 18874376 | tf_op jit(solution)/shard_map/ppermute | solution.py:557
  162.5 0.6 stack.141.mode
  163.1 0.6 pad_add_fusion.info
  163.7 17.7 %shard_map.79 = f32[2,8,128]{2,1,0:T(8,128)} custom-call(s32[2]{0:T(128)} %pad_add_fusion.info, f32[1,2,512,2048]{3,2,1,0:T(8,128)} %x_ref.7, bf16[2,2304,256]{2,1,0:T(8,128)(2,1)} %get-tuple-element.71.refs_1_.w_ref, f32[3,2,128,128]{3,2,1,0:T(8,128)} %get-tuple-element.101.s_ref, f32[7,2,128,128]{3,2,1,0:T(8,128)} %get-tuple-element.102.c_ref), custom_call_target="tpu_custom_call" | custom-call | flops 1 | bytes 1 | tf_op jit(solution)/shard_map/pallas_call | solution.py:329
  181.4 0.0 collective-permute-done.11.refs_2_
  181.4 4.6 %shard_map.80 = (f32[2,512,2048]{2,1,0:T(8,128)}, f32[2,512,1024]{2,1,0:T(8,128)}) custom-call(s32[5]{0:T(128)} %stack.141.mode, f32[2,256,2048]{2,1,0:T(8,128)} %shard_map.72.refs_0_, f32[2,256,1024]{2,1,0:T(8,128)} %get-tuple-element.99.refs_1_, f32[2,256,2048]{2,1,0:T(8,128)} %collective-permute-done.11.refs_2_, ...), custom_call_target="tpu_custom_call" | custom-call | flops 1 | bytes 1 | tf_op jit(solution)/shard_map/pallas_call | solution.py:231
  186.0 1.3 collective-permute-start.16
  187.3 0.0 copy-start.2
  187.3 5.0 %shard_map.81 = (f32[2,512,2048]{2,1,0:T(8,128)}, f32[2,512,1024]{2,1,0:T(8,128)}) custom-call(s32[5]{0:T(128)} %stack.141.mode, f32[2,256,2048]{2,1,0:T(8,128)} %shard_map.72.refs_0_, f32[2,256,1024]{2,1,0:T(8,128)} %get-tuple-element.94.refs_1_, f32[2,256,2048]{2,1,0:T(8,128)} %collective-permute-done.11.refs_2_, ...), custom_call_target="tpu_custom_call", output_to_operand_aliasing={{0}: (9, {})} | custom-call | flops 1 | bytes 1 | tf_op jit(solution)/shard_map/pallas_call | solution.py:231
  192.3 1.3 collective-permute-start.15
  193.6 0.6 slice.90
  194.2 0.5 fusion.5
  195.9 0.6 slice_multiply_fusion
  196.6 1.3 collective-permute-start.17
  197.9 4.0 %collective-permute-start.18 = (f32[3,2,128]{2,1,0:T(2,128)S(1)}, f32[3,2,128]{2,1,0:T(2,128)S(1)}, u32[]{:S(2)}, u32[]{:S(2)}) collective-permute-start(f32[3,2,128]{2,1,0:T(2,128)S(1)} %get-tuple-element.110), channel_id=1, source_target_pairs={{0,1},{1,2},{2,3},{4,5},{5,6},{6,7},{8,9},{9,10},{10,11},{12,13},{... | collective-permute-start | bytes 9224 | tf_op jit(solution)/shard_map/ppermute | solution.py:591
  201.9 0.7 collective-permute-done.18
  202.6 22.2 %collective-permute-start.19 = (f32[4,128]{1,0:T(4,128)S(1)}, f32[4,128]{1,0:T(4,128)S(1)}, u32[]{:S(2)}, u32[]{:S(2)}) collective-permute-start(f32[4,128]{1,0:T(4,128)S(1)} %slice_bitcast_fusion), channel_id=1, source_target_pairs={{0,4},{4,8},{8,12},{12,16},{16,20},{20,24},{24,28},{1,5},{5,9},{9,... | collective-permute-start | bytes 6152 | tf_op jit(solution)/shard_map/ppermute | solution.py:593
  224.8 5.1 %shard_map.82.old_ref = f32[2,512,2048]{2,1,0:T(8,128)} custom-call(s32[1]{0:T(128)} %bitcast.13.mode, f32[2,512,1024]{2,1,0:T(8,128)} %collective-permute-done.16.new_ref, f32[2,512,2048]{2,1,0:T(8,128)} %get-tuple-element.107.old_ref), custom_call_target="tpu_custom_call", output_to_operand_aliasing={{}: (2, {})} | custom-call | flops 1 | bytes 1 | tf_op jit(solution)/shard_map/pallas_call | solution.py:261
  229.9 5.1 %shard_map.83.old_ref = f32[2,512,2048]{2,1,0:T(8,128)} custom-call(s32[1]{0:T(128)} %bitcast.13.mode, f32[2,512,1024]{2,1,0:T(8,128)} %collective-permute-done.15.new_ref, f32[2,512,2048]{2,1,0:T(8,128)} %shard_map.82.old_ref), custom_call_target="tpu_custom_call", output_to_operand_aliasing={{}: (2, {})} | custom-call | flops 1 | bytes 1 | tf_op jit(solution)/shard_map/pallas_call | solution.py:261
  235.0 2.7 %shard_map.84.old_ref = f32[2,512,2048]{2,1,0:T(8,128)} custom-call(s32[1]{0:T(128)} %bitcast.mode, f32[2,128,2048]{2,1,0:T(8,128)} %collective-permute-done.9.new_ref, f32[2,512,2048]{2,1,0:T(8,128)} %shard_map.83.old_ref), custom_call_target="tpu_custom_call", output_to_operand_aliasing={{}: (2, {})} | custom-call | flops 1 | bytes 1 | tf_op jit(solution)/shard_map/pallas_call | solution.py:261
  237.7 3.2 %shard_map.85 = f32[2,512,2048]{2,1,0:T(8,128)} custom-call(s32[1]{0:T(128)} %bitcast.mode, f32[2,384,2048]{2,1,0:T(8,128)} %collective-permute-done.8.new_ref, f32[2,512,2048]{2,1,0:T(8,128)} %shard_map.84.old_ref), custom_call_target="tpu_custom_call", output_to_operand_aliasing={{}: (2, {})} | custom-call | flops 1 | bytes 1 | tf_op jit(solution)/shard_map/pallas_call | solution.py:261
  240.9 0.6 fusion.2
  (26 shorter events, 0.1 us)
Async XLA Ops:
  0.6 2.0 collective-permute-start
  8.4 70.1 %collective-permute-start.2 = (f32[2,256,2048]{2,1,0:T(8,128)}, f32[2,256,2048]{2,1,0:T(8,128)}, u32[]{:S(2)}, u32[]{:S(2)}) collective-permute-start(f32[2,256,2048]{2,1,0:T(8,128)} %get-tuple-element.69), channel_id=1, source_target_pairs={{0,8},{8,16},{16,24},{1,9},{9,17},{17,25},{2,10},{10,18},{18,26},{... | collective-permute-start | bytes 12582920 | tf_op jit(solution)/shard_map/ppermute | solution.py:518
  11.8 8.5 %collective-permute-start.1 = (s32[2]{0:T(128)S(1)}, s32[2]{0:T(128)S(1)}, u32[]{:S(2)}, u32[]{:S(2)}) collective-permute-start(s32[2]{0:T(128)S(1)} %pad_add_fusion.6), channel_id=1, source_target_pairs={{4,8},{12,16},{20,24},{8,4},{16,12},{24,20},{5,9},{13,17},{21,25},... | collective-permute-start | bytes 32 | tf_op jit(solution)/shard_map/ppermute | solution.py:520
  17.2 27.1 %collective-permute-start.3 = (f32[2,256,1024]{2,1,0:T(8,128)}, f32[2,256,1024]{2,1,0:T(8,128)}, u32[]{:S(2)}, u32[]{:S(2)}) collective-permute-start(f32[2,256,1024]{2,1,0:T(8,128)} %get-tuple-element.79), channel_id=1, source_target_pairs={{4,5},{5,4},{6,7},{7,6},{12,13},{13,12},{14,15},{15,14},{20,21},{2... | collective-permute-start | bytes 6291464 | tf_op jit(solution)/shard_map/ppermute | solution.py:481
  20.4 5.8 %copy-start.4 = (s32[2]{0:T(128)}, s32[2]{0:T(128)S(1)}, u32[]{:S(2)}) copy-start(s32[2]{0:T(128)S(1)} %collective-permute-done.1.link_bands) | copy-start | bytes 28
  26.1 27.1 %collective-permute-start.6 = (f32[2,256,1024]{2,1,0:T(8,128)}, f32[2,256,1024]{2,1,0:T(8,128)}, u32[]{:S(2)}, u32[]{:S(2)}) collective-permute-start(f32[2,256,1024]{2,1,0:T(8,128)} %get-tuple-element.88), channel_id=1, source_target_pairs={{5,7},{6,4},{13,15},{14,12},{21,23},{22,20}} | collective-permute-start | bytes 6291464 | tf_op jit(solution)/shard_map/ppermute | solution.py:481
  27.4 55.2 %collective-permute-start.4 = (f32[2,256,1024]{2,1,0:T(8,128)}, f32[2,256,1024]{2,1,0:T(8,128)}, u32[]{:S(2)}, u32[]{:S(2)}) collective-permute-start(f32[2,256,1024]{2,1,0:T(8,128)} %get-tuple-element.81), channel_id=1, source_target_pairs={{5,6},{6,5},{13,14},{14,13},{21,22},{22,21}} | collective-permute-start | bytes 6291464 | tf_op jit(solution)/shard_map/ppermute | solution.py:481
  44.3 52.4 %collective-permute-start.5 = (f32[2,256,1024]{2,1,0:T(8,128)}, f32[2,256,1024]{2,1,0:T(8,128)}, u32[]{:S(2)}, u32[]{:S(2)}) collective-permute-start(f32[2,256,1024]{2,1,0:T(8,128)} %get-tuple-element.87), channel_id=1, source_target_pairs={{4,5},{5,4},{6,7},{7,6},{12,13},{13,12},{14,15},{15,14},{20,21},{2... | collective-permute-start | bytes 6291464 | tf_op jit(solution)/shard_map/ppermute | solution.py:481
  53.2 43.5 %collective-permute-start.7 = (f32[2,256,1024]{2,1,0:T(8,128)}, f32[2,256,1024]{2,1,0:T(8,128)}, u32[]{:S(2)}, u32[]{:S(2)}) collective-permute-start(f32[2,256,1024]{2,1,0:T(8,128)} %collective-permute-done.6), channel_id=1, source_target_pairs={{7,6},{4,5},{15,14},{12,13},{23,22},{20,21}} | collective-permute-start | bytes 6291464 | tf_op jit(solution)/shard_map/ppermute | solution.py:481
  56.0 91.6 %collective-permute-start.10 = (f32[2,256,2048]{2,1,0:T(8,128)}, f32[2,256,2048]{2,1,0:T(8,128)}, u32[]{:S(2)}, u32[]{:S(2)}) collective-permute-start(f32[2,256,2048]{2,1,0:T(8,128)} %get-tuple-element.93), channel_id=1, source_target_pairs={{0,8},{8,16},{16,24},{1,9},{9,17},{17,25},{2,10},{10,18},{18,26},{... | collective-permute-start | bytes 12582920 | tf_op jit(solution)/shard_map/ppermute | solution.py:518
  120.1 27.5 %collective-permute-start.9 = (f32[2,128,2048]{2,1,0:T(8,128)}, f32[2,128,2048]{2,1,0:T(8,128)}, u32[]{:S(2)}, u32[]{:S(2)}) collective-permute-start(f32[2,128,2048]{2,1,0:T(8,128)} %shard_map.76), channel_id=1, source_target_pairs={{4,12},{12,20},{20,28},{5,13},{13,21},{21,29},{6,14},{14,22},{22,3... | collective-permute-start | bytes 6291464 | tf_op jit(solution)/shard_map/ppermute | solution.py:557
  145.0 36.4 %collective-permute-start.11 = (f32[2,256,2048]{2,1,0:T(8,128)}, f32[2,256,2048]{2,1,0:T(8,128)}, u32[]{:S(2)}, u32[]{:S(2)}) collective-permute-start(f32[2,256,2048]{2,1,0:T(8,128)} %shard_map.72.refs_0_), channel_id=1, source_target_pairs={{0,1},{1,0},{2,3},{3,2},{8,9},{9,8},{10,11},{11,10},{16,17},{17,16... | collective-permute-start | bytes 12582920 | tf_op jit(solution)/shard_map/ppermute | solution.py:481
  151.9 3.9 %collective-permute-start.12 = (f32[2,256,1024]{2,1,0:T(8,128)}, f32[2,256,1024]{2,1,0:T(8,128)}, u32[]{:S(2)}, u32[]{:S(2)}) collective-permute-start(f32[2,256,1024]{2,1,0:T(8,128)} %get-tuple-element.94.refs_1_), channel_id=1, source_target_pairs={{1,3},{2,0},{9,11},{10,8},{17,19},{18,16},{25,27},{26,24}} | collective-permute-start | bytes 6291464 | tf_op jit(solution)/shard_map/ppermute | solution.py:481
  153.8 27.6 %collective-permute-start.14 = (f32[2,256,1024]{2,1,0:T(8,128)}, f32[2,256,1024]{2,1,0:T(8,128)}, u32[]{:S(2)}, u32[]{:S(2)}) collective-permute-start(f32[2,256,1024]{2,1,0:T(8,128)} %get-tuple-element.99.refs_1_), channel_id=1, source_target_pairs={{1,2},{2,1},{9,10},{10,9},{17,18},{18,17},{25,26},{26,25}} | collective-permute-start | bytes 6291464 | tf_op jit(solution)/shard_map/ppermute | solution.py:481
  155.8 31.5 %collective-permute-start.13 = (f32[2,256,1024]{2,1,0:T(8,128)}, f32[2,256,1024]{2,1,0:T(8,128)}, u32[]{:S(2)}, u32[]{:S(2)}) collective-permute-start(f32[2,256,1024]{2,1,0:T(8,128)} %collective-permute-done.12), channel_id=1, source_target_pairs={{3,2},{0,1},{11,10},{8,9},{19,18},{16,17},{27,26},{24,25}} | collective-permute-start | bytes 6291464 | tf_op jit(solution)/shard_map/ppermute | solution.py:481
  157.8 80.0 %collective-permute-start.8 = (f32[2,384,2048]{2,1,0:T(8,128)}, f32[2,384,2048]{2,1,0:T(8,128)}, u32[]{:S(2)}, u32[]{:S(2)}) collective-permute-start(f32[2,384,2048]{2,1,0:T(8,128)} %shard_map.77), channel_id=1, source_target_pairs={{4,12},{12,20},{20,28},{5,13},{13,21},{21,29},{6,14},{14,22},{22,3... | collective-permute-start | bytes 18874376 | tf_op jit(solution)/shard_map/ppermute | solution.py:557
  186.0 38.8 %collective-permute-start.16 = (f32[2,512,1024]{2,1,0:T(8,128)}, f32[2,512,1024]{2,1,0:T(8,128)}, u32[]{:S(2)}, u32[]{:S(2)}) collective-permute-start(f32[2,512,1024]{2,1,0:T(8,128)} %get-tuple-element.106), channel_id=1, source_target_pairs={{0,4},{1,5},{2,6},{3,7}} | collective-permute-start | bytes 12582920 | tf_op jit(solution)/shard_map/ppermute | solution.py:581
  187.3 6.3 %copy-start.3 = (f32[2,128]{1,0:T(2,128)S(1)}, f32[2,128]{1,0:T(2,128)}, u32[]{:S(2)}) copy-start(f32[2,128]{1,0:T(2,128)} %get-tuple-element.98.refs_6_) | copy-start | bytes 3076
  187.3 6.9 %copy-start.2 = (f32[2,128]{1,0:T(2,128)S(1)}, f32[2,128]{1,0:T(2,128)}, u32[]{:S(2)}) copy-start(f32[2,128]{1,0:T(2,128)} %get-tuple-element.84.refs_5_) | copy-start | bytes 3076
  187.3 8.6 %copy-start.1 = (f32[2,8,128]{2,1,0:T(8,128)S(1)}, f32[2,8,128]{2,1,0:T(8,128)}, u32[]{:S(2)}) copy-start(f32[2,8,128]{2,1,0:T(8,128)} %shard_map.71) | copy-start | bytes 24580
  187.3 9.2 %copy-start = (f32[2,8,128]{2,1,0:T(8,128)S(1)}, f32[2,8,128]{2,1,0:T(8,128)}, u32[]{:S(2)}) copy-start(f32[2,8,128]{2,1,0:T(8,128)} %shard_map.79) | copy-start | bytes 24580
  192.3 37.6 %collective-permute-start.15 = (f32[2,512,1024]{2,1,0:T(8,128)}, f32[2,512,1024]{2,1,0:T(8,128)}, u32[]{:S(2)}, u32[]{:S(2)}) collective-permute-start(f32[2,512,1024]{2,1,0:T(8,128)} %get-tuple-element.105), channel_id=1, source_target_pairs={{0,4},{1,5},{2,6},{3,7}} | collective-permute-start | bytes 12582920 | tf_op jit(solution)/shard_map/ppermute | solution.py:581
  196.6 5.3 %collective-permute-start.17 = (f32[3,2,128]{2,1,0:T(2,128)S(1)}, f32[3,2,128]{2,1,0:T(2,128)S(1)}, u32[]{:S(2)}, u32[]{:S(2)}) collective-permute-start(f32[3,2,128]{2,1,0:T(2,128)S(1)} %get-tuple-element.111), channel_id=1, source_target_pairs={{1,0},{2,1},{3,2},{5,4},{6,5},{7,6},{9,8},{10,9},{11,10},{13,12},{... | collective-permute-start | bytes 9224 | tf_op jit(solution)/shard_map/ppermute | solution.py:591
  197.9 4.7 %collective-permute-start.18 = (f32[3,2,128]{2,1,0:T(2,128)S(1)}, f32[3,2,128]{2,1,0:T(2,128)S(1)}, u32[]{:S(2)}, u32[]{:S(2)}) collective-permute-start(f32[3,2,128]{2,1,0:T(2,128)S(1)} %get-tuple-element.110), channel_id=1, source_target_pairs={{0,1},{1,2},{2,3},{4,5},{5,6},{6,7},{8,9},{9,10},{10,11},{12,13},{... | collective-permute-start | bytes 9224 | tf_op jit(solution)/shard_map/ppermute | solution.py:591
  202.6 38.3 %collective-permute-start.19 = (f32[4,128]{1,0:T(4,128)S(1)}, f32[4,128]{1,0:T(4,128)S(1)}, u32[]{:S(2)}, u32[]{:S(2)}) collective-permute-start(f32[4,128]{1,0:T(4,128)S(1)} %slice_bitcast_fusion), channel_id=1, source_target_pairs={{0,4},{4,8},{8,12},{12,16},{16,20},{20,24},{24,28},{1,5},{5,9},{9,... | collective-permute-start | bytes 6152 | tf_op jit(solution)/shard_map/ppermute | solution.py:593
